TPU v7x, 512 devices: a whole 4x4x16 slice. The times are simulated.
512 devices in a mesh: gx: 16 (over z), gy: 8 (over y, core), gz: 4 (over x).
Axes of the slice: x: 4, y: 4, z: 16, core: 2. Of those that a mesh axis runs over, the one named last changes fastest.
Arguments:
- adjoint: bfloat16 [6, 32, 128, 1024], P(None, 'gz', 'gx', 'gy'), may hold values from -6 to 6
- linearized: bfloat16 [18, 32, 128, 1024], P(None, 'gz', 'gx', 'gy'), may hold values from -24 to 24
- stiffness: bfloat16 [32, 128, 1024], P('gz', 'gx', 'gy'), may hold values from 0.5 to 8
- anchor: float32 [32, 128, 1024], P('gz', 'gx', 'gy'), may hold values from 0.5 to 2
- target_tile: int32 [16, 8, 1024, 1], P('gx', 'gy'), may hold values from 0 to 127, as said below
- target_row: int32 [16, 8, 1024], P('gx', 'gy'), may hold values from 0 to 254
- target_col: int32 [16, 8, 1024], P('gx', 'gy'), may hold values from 0 to 126
- offsets: float32 [2, 16, 8, 1024], P(None, 'gx', 'gy'), may hold values from 0 to 1
Outputs:
- deformation_adjoint: float32 [3, 32, 128, 1024], P(None, 'gz', 'gx', 'gy')
- dem_gradient: float32 [2048, 2048], P('gy', 'gx')
Inputs may be any that keep to these rules, and one draw needn't show every extreme that they name: `target_tile`: A ground node of block (bx, by) names the tile of that block, bx * 8 + by, or the tile one block further along x, along y, or along both.
All inputs are finite; a program needn't handle non-finite values.
Results may differ from a plain program's by a relative error of at most 0.0005.
Values may be sent and summed in bfloat16 or wider, within the bound.
A program may use at most 64 MiB of HBM per device.

v0:
```python
import jax
import jax.numpy as jnp
from jax import lax
from jax.sharding import PartitionSpec as P

TILE_ROWS = 256
TILE_COLUMNS = 128
ITERS = 3


stabilizer = 0.25
element_bound = 2.75
spectrum_ratio = 30.0
corner_bits = (
    (0, 0, 0),
    (0, 0, 1),
    (0, 1, 0),
    (0, 1, 1),
    (1, 0, 0),
    (1, 0, 1),
    (1, 1, 0),
    (1, 1, 1),
)


def padded_2(shard, sides, width):
    for axis, dim in sides:
        peers, length = (lax.axis_size(axis), shard.shape[dim])
        up = [(i, (i + 1) % peers) for i in range(peers - 1)]
        down = [(j, i) for i, j in up]
        last = lax.slice_in_dim(shard, length - width, length, axis=dim)
        first = lax.slice_in_dim(shard, 0, width, axis=dim)
        before = lax.ppermute(last, axis, up)
        after = lax.ppermute(first, axis, down)
        shard = jnp.concatenate([before, shard, after], axis=dim)
    return shard


def passed_along(block, axis, distance):
    devices = range(lax.axis_size(axis))
    route = [(i - distance, i) for i in devices if i - distance in devices]
    return lax.ppermute(block, axis, route)


def axis_valid(first_lower, length, global_len):
    lower_ids = first_lower + jnp.arange(length, dtype=jnp.int32)
    return ((lower_ids >= 0) & (lower_ids <= global_len - 2)).astype(jnp.float32)


def box_mask(firsts, counts, totals):
    along_z = axis_valid(firsts[0], counts[0], totals[0])
    along_x = axis_valid(firsts[1], counts[1], totals[1])
    along_y = axis_valid(firsts[2], counts[2], totals[2])
    return along_z[:, None, None] * along_x[None, :, None] * along_y[None, None, :]


def corner_view(values_in, corner, extent):
    return values_in[
        :,
        corner[0] : corner[0] + extent[0],
        corner[1] : corner[1] + extent[1],
        corner[2] : corner[2] + extent[2],
    ]


def node_view(values_in, corner, extent):
    return values_in[
        :,
        1 - corner[0] : 1 - corner[0] + extent[0],
        1 - corner[1] : 1 - corner[1] + extent[1],
        1 - corner[2] : 1 - corner[2] + extent[2],
    ]


def corner_signs(corner):
    return (2.0 * corner[1] - 1.0, 2.0 * corner[2] - 1.0, 2.0 * corner[0] - 1.0)


def element_sense(node_values, linear, mask):
    extent = (node_values.shape[1] - 1, node_values.shape[2] - 1, node_values.shape[3] - 1)
    average = corner_view(node_values, corner_bits[0], extent)
    for corner in corner_bits[1:]:
        average = average + corner_view(node_values, corner, extent)
    average = average * 0.125
    senses = []
    for direction in range(3):
        summed = linear[direction].astype(jnp.float32) * average[0]
        for variable in range(1, average.shape[0]):
            summed = (
                summed + linear[3 * variable + direction].astype(jnp.float32) * average[variable]
            )
        senses.append(summed * mask)
    return jnp.stack(senses)


def transpose_gradient(element_terms, extent):
    result = jnp.zeros((3, extent[0], extent[1], extent[2]), jnp.float32)
    for corner in corner_bits:
        sign_set = corner_signs(corner)
        sign_column = jnp.array(sign_set, dtype=jnp.float32)[:, None, None, None]
        result = result + 0.25 * sign_column * node_view(element_terms, corner, extent)
    return result


def node_total(weights, extent):
    result = jnp.zeros((extent[0], extent[1], extent[2]), jnp.float32)
    for corner in corner_bits:
        result = result + node_view(weights[None], corner, extent)[0]
    return result


def node_forces(padded, weights, extent):
    elem_span = (extent[0] + 1, extent[1] + 1, extent[2] + 1)
    local_weights = weights[: elem_span[0], : elem_span[1], : elem_span[2]]
    corners = [corner_view(padded, corner, elem_span) for corner in corner_bits]
    mean_disp = corners[0]
    for position in range(1, 8):
        mean_disp = mean_disp + corners[position]
    mean_disp = mean_disp * 0.125
    gradient = []
    for direction in range(3):
        summed = 0.25 * corner_signs(corner_bits[0])[direction] * corners[0]
        for position in range(1, 8):
            summed = (
                summed + 0.25 * corner_signs(corner_bits[position])[direction] * corners[position]
            )
        gradient.append(summed)
    trace_term = gradient[0][0] + gradient[1][1] + gradient[2][2]
    stress = []
    for direction in range(3):
        stress_rows = []
        for component in range(3):
            entry_value = gradient[direction][component] + gradient[component][direction]
            if component == direction:
                entry_value = entry_value + trace_term
            stress_rows.append(local_weights * entry_value)
        stress.append(jnp.stack(stress_rows))
    result = jnp.zeros((3, extent[0], extent[1], extent[2]), jnp.float32)
    for position in range(8):
        sign_set = corner_signs(corner_bits[position])
        corner_force = 0.25 * (
            sign_set[0] * stress[0] + sign_set[1] * stress[1] + sign_set[2] * stress[2]
        )
        corner_force = corner_force + stabilizer * local_weights * (corners[position] - mean_disp)
        result = result + node_view(corner_force, corner_bits[position], extent)
    return result


def per_device(
    adjoint, linearized, stiffness, anchor, target_tile, target_row, target_col, offsets
):
    extent = (adjoint.shape[1], adjoint.shape[2], adjoint.shape[3])
    totals = (
        extent[0] * lax.axis_size("gz"),
        extent[1] * lax.axis_size("gx"),
        extent[2] * lax.axis_size("gy"),
    )
    starts = (
        lax.axis_index("gz") * extent[0],
        lax.axis_index("gx") * extent[1],
        lax.axis_index("gy") * extent[2],
    )
    rim_firsts = (starts[0] - 1, starts[1] - 1, starts[2] - 1)
    variables = adjoint.shape[0]
    stacked = jnp.concatenate([adjoint, stiffness[None]], axis=0)
    padded = padded_2(stacked, (("gx", 2), ("gy", 3), ("gz", 1)), 1)
    node_values = padded[:variables].astype(jnp.float32)
    raw_weights = padded[variables].astype(jnp.float32)
    local_terms = element_sense(
        node_values[:, 1:, 1:, 1:], linearized, box_mask(starts, extent, totals)
    )
    from_lower_x = passed_along(local_terms[:, :, -1:, :], "gx", 1)
    local_terms = jnp.concatenate([from_lower_x, local_terms], axis=2)
    from_lower_y = passed_along(local_terms[:, :, :, -1:], "gy", 1)
    local_terms = jnp.concatenate([from_lower_y, local_terms], axis=3)
    from_lower_z = passed_along(local_terms[:, -1:, :, :], "gz", 1)
    element_terms = jnp.concatenate([from_lower_z, local_terms], axis=1)
    coordinate_gradient = transpose_gradient(element_terms, extent)
    padded_span = (extent[0] + 2, extent[1] + 2, extent[2] + 2)
    weights = raw_weights * box_mask(rim_firsts, padded_span, totals)
    local_bound = jnp.max(anchor + element_bound * node_total(weights, extent))
    top_bound = lax.pmax(local_bound, ("gx", "gy", "gz"))

    def apply_operator(nodal):
        padded_field = padded_2(nodal, (("gx", 2), ("gy", 3), ("gz", 1)), 1)
        return anchor[None] * nodal + node_forces(padded_field, weights, extent)

    low_bound = top_bound / spectrum_ratio
    center = 0.5 * (top_bound + low_bound)
    half_width = 0.5 * (top_bound - low_bound)
    ratio_term = center / half_width
    rho_now = 1.0 / ratio_term
    deformation_adjoint = jnp.zeros_like(coordinate_gradient)
    residual = coordinate_gradient
    first_applied = apply_operator(residual / center)
    direction = residual / center
    for sweep_step in range(ITERS):
        if sweep_step == 0:
            applied = first_applied
        else:
            applied = apply_operator(direction)
        deformation_adjoint = deformation_adjoint + direction
        residual = residual - applied
        rho_next = 1.0 / (2.0 * ratio_term - rho_now)
        direction = rho_next * rho_now * direction + 2.0 * rho_next / half_width * residual
        rho_now = rho_next
    levels = (lax.axis_index("gz") * extent[0] + jnp.arange(extent[0], dtype=jnp.int32)).astype(
        jnp.float32
    )
    blending = (totals[0] - 1 - levels) / (totals[0] - 1)
    column = jnp.sum(blending[:, None, None] * deformation_adjoint[2], axis=0).reshape(-1)
    column = lax.psum(column, "gz")
    tile_ids = target_tile.reshape(-1)
    size_gy = lax.axis_size("gy")
    row_step = tile_ids % size_gy - lax.axis_index("gy")
    col_step = tile_ids // size_gy - lax.axis_index("gx")
    row_local = target_row.reshape(-1)
    col_local = target_col.reshape(-1)
    row_fraction = offsets[0].reshape(-1)
    column_fraction = offsets[1].reshape(-1)
    weighted_contribution = jnp.stack(
        [
            column * ((1.0 - row_fraction) * (1.0 - column_fraction)),
            column * ((1.0 - row_fraction) * column_fraction),
            column * (row_fraction * (1.0 - column_fraction)),
            column * (row_fraction * column_fraction),
        ],
        axis=0,
    )
    flattened_location = (
        (row_step * TILE_ROWS + row_local) * (2 * TILE_COLUMNS)
        + col_step * TILE_COLUMNS
        + col_local
    )
    elevation_grid = jnp.zeros((4 * TILE_ROWS * TILE_COLUMNS,), jnp.float32)
    elevation_grid = elevation_grid.at[flattened_location].add(weighted_contribution[0])
    elevation_grid = elevation_grid.at[flattened_location + 1].add(weighted_contribution[1])
    elevation_grid = elevation_grid.at[flattened_location + 2 * TILE_COLUMNS].add(
        weighted_contribution[2]
    )
    elevation_grid = elevation_grid.at[flattened_location + 2 * TILE_COLUMNS + 1].add(
        weighted_contribution[3]
    )
    elevation_grid = elevation_grid.reshape(2, TILE_ROWS, 2, TILE_COLUMNS)
    pieces = [
        elevation_grid[0, :, 0, :],
        elevation_grid[0, :, 1, :],
        elevation_grid[1, :, 0, :],
        elevation_grid[1, :, 1, :],
    ]
    row_in = passed_along(pieces[2], "gy", 1)
    column_in = passed_along(pieces[1], "gx", 1)
    corner_mid = passed_along(pieces[3], "gx", 1)
    corner_in = passed_along(corner_mid, "gy", 1)
    arrived = [row_in, column_in, corner_in]
    tile_out = pieces[0] + arrived[0] + arrived[1] + arrived[2]
    return (deformation_adjoint, tile_out)


def solution(mesh):
    in_specs = (
        P(None, "gz", "gx", "gy"),
        P(None, "gz", "gx", "gy"),
        P("gz", "gx", "gy"),
        P("gz", "gx", "gy"),
        P("gx", "gy", None, None),
        P("gx", "gy", None),
        P("gx", "gy", None),
        P(None, "gx", "gy", None),
    )
    out_specs = (P(None, "gz", "gx", "gy"), P("gy", "gx"))
    return jax.shard_map(
        per_device, mesh=mesh, in_specs=in_specs, out_specs=out_specs, check_vma=False
    )
```

profile of v0, /device:TPU:1, one launch (start us, length us, event | category | flops | bytes accessed | tf_op | source)
XLA Modules:
  0.0 268.9 jit_solution(5852782878996299264)
XLA Ops:
  0.7 1.1 pad_maximum_fusion.39
  1.7 4.4 %collective-permute-start = (bf16[7,8,1,128]{3,2,1,0:T(2,128)(2,1)S(1)}, bf16[7,8,1,128]{3,2,1,0:T(2,128)(2,1)S(1)}, u32[]{:S(2)}, u32[]{:S(2)}) collective-permute-start(bf16[7,8,1,128]{3,2,1,0:T(2,128)(2,1)S(1)} %get-tuple-element.87), channel_id=1, source_target_pairs={{0,32},{32,64},{64,96},{96,128},{128,160},{160,192},{192,224},{224... | collective-permute-start | bytes 43016 | tf_op jit(solution)/shard_map/ppermute | solution.py:33
  6.1 1.3 collective-permute-start.1
  7.5 3.4 %collective-permute-done.1 = bf16[7,8,1,128]{3,2,1,0:T(2,128)(2,1)S(1)} collective-permute-done((bf16[7,8,1,128]{3,2,1,0:T(2,128)(2,1)S(1)}, bf16[7,8,1,128]{3,2,1,0:T(2,128)(2,1)S(1)}, u32[]{:S(2)}, u32[]{:S(2)}) %collective-permute-start.1) | collective-permute-done | bytes 14368 | tf_op jit(solution)/shard_map/ppermute | solution.py:34
  10.9 1.0 pad_maximum_fusion.9
  12.1 5.0 %collective-permute-start.2 = (bf16[7,8,10,1]{3,2,1,0:T(8,128)(2,1)S(1)}, bf16[7,8,10,1]{3,2,1,0:T(8,128)(2,1)S(1)}, u32[]{:S(2)}, u32[]{:S(2)}) collective-permute-start(bf16[7,8,10,1]{3,2,1,0:T(8,128)(2,1)S(1)} %get-tuple-element.72), channel_id=1, source_target_pairs={{0,4},{4,8},{8,12},{12,16},{16,20},{20,24},{24,28},{1,5},{5,9},{9,... | collective-permute-start | bytes 3368 | tf_op jit(solution)/shard_map/ppermute | solution.py:33
  17.1 3.0 %collective-permute-start.3 = (bf16[7,8,10,1]{3,2,1,0:T(8,128)(2,1)S(1)}, bf16[7,8,10,1]{3,2,1,0:T(8,128)(2,1)S(1)}, u32[]{:S(2)}, u32[]{:S(2)}) collective-permute-start(bf16[7,8,10,1]{3,2,1,0:T(8,128)(2,1)S(1)} %get-tuple-element.73), channel_id=1, source_target_pairs={{4,0},{8,4},{12,8},{16,12},{20,16},{24,20},{28,24},{5,1},{9,5},{13... | collective-permute-start | bytes 3368 | tf_op jit(solution)/shard_map/ppermute | solution.py:34
  20.2 4.3 %collective-permute-done.3 = bf16[7,8,10,1]{3,2,1,0:T(8,128)(2,1)S(1)} collective-permute-done((bf16[7,8,10,1]{3,2,1,0:T(8,128)(2,1)S(1)}, bf16[7,8,10,1]{3,2,1,0:T(8,128)(2,1)S(1)}, u32[]{:S(2)}, u32[]{:S(2)}) %collective-permute-start.3) | collective-permute-done | bytes 1152 | tf_op jit(solution)/shard_map/ppermute | solution.py:34
  24.6 3.1 %collective-permute-start.4 = (bf16[7,1,10,130]{3,2,1,0:T(8,128)(2,1)S(1)}, bf16[7,1,10,130]{3,2,1,0:T(8,128)(2,1)S(1)}, u32[]{:S(2)}, u32[]{:S(2)}) collective-permute-start(bf16[7,1,10,130]{3,2,1,0:T(8,128)(2,1)S(1)} %get-tuple-element.32), channel_id=1, source_target_pairs={{0,1},{1,2},{2,3},{4,5},{5,6},{6,7},{8,9},{9,10},{10,11},{12,13},{... | collective-permute-start | bytes 54608 | tf_op jit(solution)/shard_map/ppermute | solution.py:33
  27.8 1.3 collective-permute-start.5
  29.1 3.6 %collective-permute-done.5 = bf16[7,1,10,130]{3,2,1,0:T(8,128)(2,1)S(1)} collective-permute-done((bf16[7,1,10,130]{3,2,1,0:T(8,128)(2,1)S(1)}, bf16[7,1,10,130]{3,2,1,0:T(8,128)(2,1)S(1)}, u32[]{:S(2)}, u32[]{:S(2)}) %collective-permute-start.5) | collective-permute-done | bytes 18232 | tf_op jit(solution)/shard_map/ppermute | solution.py:34
  32.7 0.5 pad_maximum_fusion
  33.3 0.5 fusion.2
  33.8 0.5 copy-done.2
  34.6 3.5 %collective-permute-start.6 = (f32[3,8,1,128]{3,2,1,0:T(1,128)S(1)}, f32[3,8,1,128]{3,2,1,0:T(1,128)S(1)}, u32[]{:S(2)}, u32[]{:S(2)}) collective-permute-start(f32[3,8,1,128]{3,2,1,0:T(1,128)S(1)} %slice.591), channel_id=1, source_target_pairs={{0,32},{32,64},{64,96},{96,128},{128,160},{160,192},{192,224},{224... | collective-permute-start | bytes 36872 | tf_op jit(solution)/shard_map/ppermute | solution.py:42
  38.2 0.8 collective-permute-done.6
  39.1 4.1 %collective-permute-start.7 = (f32[3,8,9,1]{3,2,1,0:T(8,128)S(1)}, f32[3,8,9,1]{3,2,1,0:T(8,128)S(1)}, u32[]{:S(2)}, u32[]{:S(2)}) collective-permute-start(f32[3,8,9,1]{3,2,1,0:T(8,128)S(1)} %slice.592), channel_id=1, source_target_pairs={{0,4},{4,8},{8,12},{12,16},{16,20},{20,24},{24,28},{1,5},{5,9},{9,... | collective-permute-start | bytes 2600 | tf_op jit(solution)/shard_map/ppermute | solution.py:42
  43.4 2.5 collective-permute-done.7
  46.0 3.1 %collective-permute-start.8 = (f32[3,1,9,129]{3,2,1,0:T(8,128)S(1)}, f32[3,1,9,129]{3,2,1,0:T(8,128)S(1)}, u32[]{:S(2)}, u32[]{:S(2)}) collective-permute-start(f32[3,1,9,129]{3,2,1,0:T(8,128)S(1)} %pad_maximum_fusion.34), channel_id=1, source_target_pairs={{0,1},{1,2},{2,3},{4,5},{5,6},{6,7},{8,9},{9,10},{10,11},{12,13},{... | collective-permute-start | bytes 41804 | tf_op jit(solution)/shard_map/ppermute | solution.py:42
  49.1 0.7 fusion.111
  49.8 110.0 %pmax.7 = f32[]{:T(128)} all-reduce(f32[]{:T(128)} %fusion.111), channel_id=1, replica_groups=mesh['gx'=16,'gy'=8,'gz'=4] {'gx','gy','gz'}, use_global_device_ids=true, to_apply=%region_1.0 | all-reduce | flops 1 | bytes 8 | tf_op jit(solution)/shard_map/pmax | solution.py:182
  161.2 0.3 broadcast_divide_fusion
  161.6 1.3 collective-permute-start.10
  162.9 4.0 %collective-permute-start.9 = (f32[3,8,1,128]{3,2,1,0:T(1,128)S(1)}, f32[3,8,1,128]{3,2,1,0:T(1,128)S(1)}, u32[]{:S(2)}, u32[]{:S(2)}) collective-permute-start(f32[3,8,1,128]{3,2,1,0:T(1,128)S(1)} %get-tuple-element.91), channel_id=1, source_target_pairs={{0,32},{32,64},{64,96},{96,128},{128,160},{160,192},{192,224},{224... | collective-permute-start | bytes 36872 | tf_op jit(solution)/shard_map/ppermute | solution.py:33
  166.9 0.8 collective-permute-done.9
  167.9 2.7 %collective-permute-start.11 = (f32[3,8,10,1]{3,2,1,0:T(8,128)S(1)}, f32[3,8,10,1]{3,2,1,0:T(8,128)S(1)}, u32[]{:S(2)}, u32[]{:S(2)}) collective-permute-start(f32[3,8,10,1]{3,2,1,0:T(8,128)S(1)} %get-tuple-element.76), channel_id=1, source_target_pairs={{0,4},{4,8},{8,12},{12,16},{16,20},{20,24},{24,28},{1,5},{5,9},{9,... | collective-permute-start | bytes 2888 | tf_op jit(solution)/shard_map/ppermute | solution.py:33
  170.6 2.8 %collective-permute-start.12 = (f32[3,8,10,1]{3,2,1,0:T(8,128)S(1)}, f32[3,8,10,1]{3,2,1,0:T(8,128)S(1)}, u32[]{:S(2)}, u32[]{:S(2)}) collective-permute-start(f32[3,8,10,1]{3,2,1,0:T(8,128)S(1)} %get-tuple-element.77), channel_id=1, source_target_pairs={{4,0},{8,4},{12,8},{16,12},{20,16},{24,20},{28,24},{5,1},{9,5},{13... | collective-permute-start | bytes 2888 | tf_op jit(solution)/shard_map/ppermute | solution.py:34
  173.5 4.0 %collective-permute-done.12 = f32[3,8,10,1]{3,2,1,0:T(8,128)S(1)} collective-permute-done((f32[3,8,10,1]{3,2,1,0:T(8,128)S(1)}, f32[3,8,10,1]{3,2,1,0:T(8,128)S(1)}, u32[]{:S(2)}, u32[]{:S(2)}) %collective-permute-start.12) | collective-permute-done | bytes 992 | tf_op jit(solution)/shard_map/ppermute | solution.py:34
  177.7 2.7 %collective-permute-start.13 = (f32[3,1,10,130]{3,2,1,0:T(8,128)S(1)}, f32[3,1,10,130]{3,2,1,0:T(8,128)S(1)}, u32[]{:S(2)}, u32[]{:S(2)}) collective-permute-start(f32[3,1,10,130]{3,2,1,0:T(8,128)S(1)} %get-tuple-element.44), channel_id=1, source_target_pairs={{0,1},{1,2},{2,3},{4,5},{5,6},{6,7},{8,9},{9,10},{10,11},{12,13},{... | collective-permute-start | bytes 46808 | tf_op jit(solution)/shard_map/ppermute | solution.py:33
  180.4 1.3 collective-permute-start.14
  182.6 2.7 collective-permute-done.14
  185.3 0.6 maximum_maximum_fusion
  185.8 0.7 add_add_fusion.4
  186.5 0.6 add_add_fusion.3
  187.2 0.2 fusion.119
  187.6 0.2 multiply_add_fusion.6
  188.1 0.5 multiply_add_fusion.8
  188.7 3.9 %collective-permute-start.15 = (f32[3,8,1,128]{3,2,1,0:T(1,128)S(1)}, f32[3,8,1,128]{3,2,1,0:T(1,128)S(1)}, u32[]{:S(2)}, u32[]{:S(2)}) collective-permute-start(f32[3,8,1,128]{3,2,1,0:T(1,128)S(1)} %get-tuple-element.89), channel_id=1, source_target_pairs={{0,32},{32,64},{64,96},{96,128},{128,160},{160,192},{192,224},{224... | collective-permute-start | bytes 36872 | tf_op jit(solution)/shard_map/ppermute | solution.py:33
  192.6 1.3 collective-permute-start.16
  193.9 3.1 %collective-permute-done.16 = f32[3,8,1,128]{3,2,1,0:T(1,128)S(1)} collective-permute-done((f32[3,8,1,128]{3,2,1,0:T(1,128)S(1)}, f32[3,8,1,128]{3,2,1,0:T(1,128)S(1)}, u32[]{:S(2)}, u32[]{:S(2)}) %collective-permute-start.16) | collective-permute-done | bytes 12320 | tf_op jit(solution)/shard_map/ppermute | solution.py:34
  197.2 4.8 %collective-permute-start.17 = (f32[3,8,10,1]{3,2,1,0:T(8,128)S(1)}, f32[3,8,10,1]{3,2,1,0:T(8,128)S(1)}, u32[]{:S(2)}, u32[]{:S(2)}) collective-permute-start(f32[3,8,10,1]{3,2,1,0:T(8,128)S(1)} %get-tuple-element.74), channel_id=1, source_target_pairs={{0,4},{4,8},{8,12},{12,16},{16,20},{20,24},{24,28},{1,5},{5,9},{9,... | collective-permute-start | bytes 2888 | tf_op jit(solution)/shard_map/ppermute | solution.py:33
  202.0 1.9 collective-permute-start.18
  203.9 0.6 collective-permute-done.17
  204.6 4.4 %collective-permute-done.18 = f32[3,8,10,1]{3,2,1,0:T(8,128)S(1)} collective-permute-done((f32[3,8,10,1]{3,2,1,0:T(8,128)S(1)}, f32[3,8,10,1]{3,2,1,0:T(8,128)S(1)}, u32[]{:S(2)}, u32[]{:S(2)}) %collective-permute-start.18) | collective-permute-done | bytes 992 | tf_op jit(solution)/shard_map/ppermute | solution.py:34
  209.1 3.4 %collective-permute-start.19 = (f32[3,1,10,130]{3,2,1,0:T(8,128)S(1)}, f32[3,1,10,130]{3,2,1,0:T(8,128)S(1)}, u32[]{:S(2)}, u32[]{:S(2)}) collective-permute-start(f32[3,1,10,130]{3,2,1,0:T(8,128)S(1)} %get-tuple-element.40), channel_id=1, source_target_pairs={{0,1},{1,2},{2,3},{4,5},{5,6},{6,7},{8,9},{9,10},{10,11},{12,13},{... | collective-permute-start | bytes 46808 | tf_op jit(solution)/shard_map/ppermute | solution.py:33
  212.5 1.3 collective-permute-start.20
  213.9 3.4 %collective-permute-done.20 = f32[3,1,10,130]{3,2,1,0:T(8,128)S(1)} collective-permute-done((f32[3,1,10,130]{3,2,1,0:T(8,128)S(1)}, f32[3,1,10,130]{3,2,1,0:T(8,128)S(1)}, u32[]{:S(2)}, u32[]{:S(2)}) %collective-permute-start.20) | collective-permute-done | bytes 15632 | tf_op jit(solution)/shard_map/ppermute | solution.py:34
  217.3 0.6 maximum_maximum_fusion.1
  217.9 0.7 add_add_fusion.1
  218.5 0.6 add_add_fusion
  219.2 0.2 fusion.118
  220.0 0.5 fusion.34
  220.6 7.3 %psum.7 = f32[1024]{0:T(1024)S(1)} all-reduce(f32[1024]{0:T(1024)S(1)} %bitcast.161), channel_id=1, replica_groups=mesh['gx'=16,'gy'=8,'gz'=4] {'gz'}, use_global_device_ids=true, to_apply=%region_3.0 | all-reduce | flops 1024 | bytes 8192 | tf_op jit(solution)/shard_map/psum | solution.py:212
  227.9 6.1 %scatter_custom_fusion = f32[131072]{0:T(1024)S(1)} fusion(s32[1024]{0:T(1024)S(1)} %bitcast.164, f32[1024]{0:T(1024)S(1)} %get-tuple-element.96, f32[]{:T(128)} %constant.113.clone.1), kind=kCustom, calls=%fused_computation.32 | custom fusion | flops 1024 | bytes 524292 | tf_op jit(solution)/shard_map/scatter-add | solution.py:236
  234.0 6.3 %scatter_fusion = f32[131072]{0:T(1024)S(1)} fusion(f32[131072]{0:T(1024)S(1)} %scatter_custom_fusion, s32[1024]{0:T(1024)S(1)} %bitcast.160, f32[1024]{0:T(1024)S(1)} %get-tuple-element.95), kind=kCustom, calls=%fused_computation.1 | custom fusion | flops 1024 | bytes 16384 | tf_op jit(solution)/shard_map/scatter-add | solution.py:237
  240.3 6.3 %scatter_fusion.1 = f32[131072]{0:T(1024)S(1)} fusion(f32[131072]{0:T(1024)S(1)} %scatter_fusion, s32[1024]{0:T(1024)S(1)} %bitcast.159, f32[1024]{0:T(1024)S(1)} %get-tuple-element.94), kind=kCustom, calls=%fused_computation.2 | custom fusion | flops 1024 | bytes 16384 | tf_op jit(solution)/shard_map/scatter-add | solution.py:238
  246.6 6.3 %scatter_fusion.2 = f32[131072]{0:T(1024)S(1)} fusion(f32[131072]{0:T(1024)S(1)} %scatter_fusion.1, s32[1024]{0:T(1024)S(1)} %bitcast.158, f32[1024]{0:T(1024)S(1)} %get-tuple-element.93), kind=kCustom, calls=%fused_computation.3 | custom fusion | flops 1024 | bytes 16384 | tf_op jit(solution)/shard_map/scatter-add | solution.py:241
  252.8 0.4 fusion.117
  253.2 1.6 collective-permute-start.23
  254.9 5.5 %collective-permute-start.21 = (f32[256,128]{1,0:T(8,128)S(1)}, f32[256,128]{1,0:T(8,128)S(1)}, u32[]{:S(2)}, u32[]{:S(2)}) collective-permute-start(f32[256,128]{1,0:T(8,128)S(1)} %bitcast.152), channel_id=1, source_target_pairs={{0,4},{4,8},{8,12},{12,16},{16,20},{20,24},{24,28},{1,5},{5,9},{9,... | collective-permute-start | bytes 393224 | tf_op jit(solution)/shard_map/ppermute | solution.py:42
  260.4 3.7 %collective-permute-start.22 = (f32[256,128]{1,0:T(8,128)S(1)}, f32[256,128]{1,0:T(8,128)S(1)}, u32[]{:S(2)}, u32[]{:S(2)}) collective-permute-start(f32[256,128]{1,0:T(8,128)S(1)} %bitcast.151), channel_id=1, source_target_pairs={{0,32},{32,64},{64,96},{96,128},{128,160},{160,192},{192,224},{224... | collective-permute-start | bytes 393224 | tf_op jit(solution)/shard_map/ppermute | solution.py:42
  264.0 2.2 collective-permute-start.24
  266.3 1.9 collective-permute-done.24
  268.2 0.7 add_add_fusion.8
  (82 shorter events, 3.1 us)
Async XLA Ops:
  0.6 23.8 %copy-start.3 = (bf16[8,8,128]{2,1,0:T(8,128)(2,1)S(1)}, bf16[8,8,128]{2,1,0:T(8,128)(2,1)}, u32[]{:S(2)}) copy-start(bf16[8,8,128]{2,1,0:T(8,128)(2,1)} %param.18) | copy-start | bytes 49156
  0.6 23.8 %copy-start = (bf16[6,8,8,128]{3,2,1,0:T(8,128)(2,1)S(1)}, bf16[6,8,8,128]{3,2,1,0:T(8,128)(2,1)}, u32[]{:S(2)}) copy-start(bf16[6,8,8,128]{3,2,1,0:T(8,128)(2,1)} %param.16) | copy-start | bytes 294916
  1.7 5.8 %collective-permute-start = (bf16[7,8,1,128]{3,2,1,0:T(2,128)(2,1)S(1)}, bf16[7,8,1,128]{3,2,1,0:T(2,128)(2,1)S(1)}, u32[]{:S(2)}, u32[]{:S(2)}) collective-permute-start(bf16[7,8,1,128]{3,2,1,0:T(2,128)(2,1)S(1)} %get-tuple-element.87), channel_id=1, source_target_pairs={{0,32},{32,64},{64,96},{96,128},{128,160},{160,192},{192,224},{224... | collective-permute-start | bytes 43016 | tf_op jit(solution)/shard_map/ppermute | solution.py:33
  6.1 4.8 %collective-permute-start.1 = (bf16[7,8,1,128]{3,2,1,0:T(2,128)(2,1)S(1)}, bf16[7,8,1,128]{3,2,1,0:T(2,128)(2,1)S(1)}, u32[]{:S(2)}, u32[]{:S(2)}) collective-permute-start(bf16[7,8,1,128]{3,2,1,0:T(2,128)(2,1)S(1)} %get-tuple-element.88), channel_id=1, source_target_pairs={{32,0},{64,32},{96,64},{128,96},{160,128},{192,160},{224,192},{256... | collective-permute-start | bytes 43016 | tf_op jit(solution)/shard_map/ppermute | solution.py:34
  12.1 8.1 %collective-permute-start.2 = (bf16[7,8,10,1]{3,2,1,0:T(8,128)(2,1)S(1)}, bf16[7,8,10,1]{3,2,1,0:T(8,128)(2,1)S(1)}, u32[]{:S(2)}, u32[]{:S(2)}) collective-permute-start(bf16[7,8,10,1]{3,2,1,0:T(8,128)(2,1)S(1)} %get-tuple-element.72), channel_id=1, source_target_pairs={{0,4},{4,8},{8,12},{12,16},{16,20},{20,24},{24,28},{1,5},{5,9},{9,... | collective-permute-start | bytes 3368 | tf_op jit(solution)/shard_map/ppermute | solution.py:33
  17.1 7.3 %collective-permute-start.3 = (bf16[7,8,10,1]{3,2,1,0:T(8,128)(2,1)S(1)}, bf16[7,8,10,1]{3,2,1,0:T(8,128)(2,1)S(1)}, u32[]{:S(2)}, u32[]{:S(2)}) collective-permute-start(bf16[7,8,10,1]{3,2,1,0:T(8,128)(2,1)S(1)} %get-tuple-element.73), channel_id=1, source_target_pairs={{4,0},{8,4},{12,8},{16,12},{20,16},{24,20},{28,24},{5,1},{9,5},{13... | collective-permute-start | bytes 3368 | tf_op jit(solution)/shard_map/ppermute | solution.py:34
  24.6 4.4 %collective-permute-start.4 = (bf16[7,1,10,130]{3,2,1,0:T(8,128)(2,1)S(1)}, bf16[7,1,10,130]{3,2,1,0:T(8,128)(2,1)S(1)}, u32[]{:S(2)}, u32[]{:S(2)}) collective-permute-start(bf16[7,1,10,130]{3,2,1,0:T(8,128)(2,1)S(1)} %get-tuple-element.32), channel_id=1, source_target_pairs={{0,1},{1,2},{2,3},{4,5},{5,6},{6,7},{8,9},{9,10},{10,11},{12,13},{... | collective-permute-start | bytes 54608 | tf_op jit(solution)/shard_map/ppermute | solution.py:33
  27.8 4.9 %collective-permute-start.5 = (bf16[7,1,10,130]{3,2,1,0:T(8,128)(2,1)S(1)}, bf16[7,1,10,130]{3,2,1,0:T(8,128)(2,1)S(1)}, u32[]{:S(2)}, u32[]{:S(2)}) collective-permute-start(bf16[7,1,10,130]{3,2,1,0:T(8,128)(2,1)S(1)} %get-tuple-element.33), channel_id=1, source_target_pairs={{1,0},{2,1},{3,2},{5,4},{6,5},{7,6},{9,8},{10,9},{11,10},{13,12},{... | collective-permute-start | bytes 54608 | tf_op jit(solution)/shard_map/ppermute | solution.py:34
  33.3 1.0 copy-start.2
  34.5 14.6 %copy-start.1 = (f32[8,8,128]{2,1,0:T(8,128)S(1)}, f32[8,8,128]{2,1,0:T(8,128)}, u32[]{:S(2)}) copy-start(f32[8,8,128]{2,1,0:T(8,128)} %param.19) | copy-start | bytes 98308
  34.5 126.6 %copy-start.9 = (f32[3]{0:T(128)S(1)}, f32[3]{0:T(128)}, u32[]{:S(2)}) copy-start(f32[3]{0:T(128)} %constant.142) | copy-start | bytes 40
  34.6 126.6 %copy-start.10 = (f32[3]{0:T(128)S(1)}, f32[3]{0:T(128)}, u32[]{:S(2)}) copy-start(f32[3]{0:T(128)} %constant.143) | copy-start | bytes 40
  34.6 126.6 %copy-start.11 = (f32[3]{0:T(128)S(1)}, f32[3]{0:T(128)}, u32[]{:S(2)}) copy-start(f32[3]{0:T(128)} %constant.144) | copy-start | bytes 40
  34.6 126.6 %copy-start.12 = (f32[3]{0:T(128)S(1)}, f32[3]{0:T(128)}, u32[]{:S(2)}) copy-start(f32[3]{0:T(128)} %constant.145) | copy-start | bytes 40
  34.6 126.6 %copy-start.13 = (f32[3]{0:T(128)S(1)}, f32[3]{0:T(128)}, u32[]{:S(2)}) copy-start(f32[3]{0:T(128)} %constant.146) | copy-start | bytes 40
  34.6 126.6 %copy-start.14 = (f32[3]{0:T(128)S(1)}, f32[3]{0:T(128)}, u32[]{:S(2)}) copy-start(f32[3]{0:T(128)} %constant.147) | copy-start | bytes 40
  34.6 4.4 %collective-permute-start.6 = (f32[3,8,1,128]{3,2,1,0:T(1,128)S(1)}, f32[3,8,1,128]{3,2,1,0:T(1,128)S(1)}, u32[]{:S(2)}, u32[]{:S(2)}) collective-permute-start(f32[3,8,1,128]{3,2,1,0:T(1,128)S(1)} %slice.591), channel_id=1, source_target_pairs={{0,32},{32,64},{64,96},{96,128},{128,160},{160,192},{192,224},{224... | collective-permute-start | bytes 36872 | tf_op jit(solution)/shard_map/ppermute | solution.py:42
  39.1 6.7 %collective-permute-start.7 = (f32[3,8,9,1]{3,2,1,0:T(8,128)S(1)}, f32[3,8,9,1]{3,2,1,0:T(8,128)S(1)}, u32[]{:S(2)}, u32[]{:S(2)}) collective-permute-start(f32[3,8,9,1]{3,2,1,0:T(8,128)S(1)} %slice.592), channel_id=1, source_target_pairs={{0,4},{4,8},{8,12},{12,16},{16,20},{20,24},{24,28},{1,5},{5,9},{9,... | collective-permute-start | bytes 2600 | tf_op jit(solution)/shard_map/ppermute | solution.py:42
  46.0 115.2 %collective-permute-start.8 = (f32[3,1,9,129]{3,2,1,0:T(8,128)S(1)}, f32[3,1,9,129]{3,2,1,0:T(8,128)S(1)}, u32[]{:S(2)}, u32[]{:S(2)}) collective-permute-start(f32[3,1,9,129]{3,2,1,0:T(8,128)S(1)} %pad_maximum_fusion.34), channel_id=1, source_target_pairs={{0,1},{1,2},{2,3},{4,5},{5,6},{6,7},{8,9},{9,10},{10,11},{12,13},{... | collective-permute-start | bytes 41804 | tf_op jit(solution)/shard_map/ppermute | solution.py:42
  49.8 123.6 %copy-start.6 = (s32[1,1,1024]{2,1,0:T(1,128)S(1)}, s32[1,1,1024]{2,1,0:T(1,128)}, u32[]{:S(2)}) copy-start(s32[1,1,1024]{2,1,0:T(1,128)} %param.22) | copy-start | bytes 12292
  49.8 123.6 %copy-start.7 = (s32[1,1,1024]{2,1,0:T(1,128)S(1)}, s32[1,1,1024]{2,1,0:T(1,128)}, u32[]{:S(2)}) copy-start(s32[1,1,1024]{2,1,0:T(1,128)} %param.21) | copy-start | bytes 12292
  49.8 123.7 %copy-start.8 = (s32[1,1,1024,1]{2,3,1,0:T(1,128)S(1)}, s32[1,1,1024,1]{2,3,1,0:T(1,128)}, u32[]{:S(2)}) copy-start(s32[1,1,1024,1]{2,3,1,0:T(1,128)} %param.20) | copy-start | bytes 12292
  161.6 5.3 %collective-permute-start.10 = (f32[3,8,1,128]{3,2,1,0:T(1,128)S(1)}, f32[3,8,1,128]{3,2,1,0:T(1,128)S(1)}, u32[]{:S(2)}, u32[]{:S(2)}) collective-permute-start(f32[3,8,1,128]{3,2,1,0:T(1,128)S(1)} %get-tuple-element.92), channel_id=1, source_target_pairs={{32,0},{64,32},{96,64},{128,96},{160,128},{192,160},{224,192},{256... | collective-permute-start | bytes 36872 | tf_op jit(solution)/shard_map/ppermute | solution.py:34
  162.9 4.8 %collective-permute-start.9 = (f32[3,8,1,128]{3,2,1,0:T(1,128)S(1)}, f32[3,8,1,128]{3,2,1,0:T(1,128)S(1)}, u32[]{:S(2)}, u32[]{:S(2)}) collective-permute-start(f32[3,8,1,128]{3,2,1,0:T(1,128)S(1)} %get-tuple-element.91), channel_id=1, source_target_pairs={{0,32},{32,64},{64,96},{96,128},{128,160},{160,192},{192,224},{224... | collective-permute-start | bytes 36872 | tf_op jit(solution)/shard_map/ppermute | solution.py:33
  167.9 5.7 %collective-permute-start.11 = (f32[3,8,10,1]{3,2,1,0:T(8,128)S(1)}, f32[3,8,10,1]{3,2,1,0:T(8,128)S(1)}, u32[]{:S(2)}, u32[]{:S(2)}) collective-permute-start(f32[3,8,10,1]{3,2,1,0:T(8,128)S(1)} %get-tuple-element.76), channel_id=1, source_target_pairs={{0,4},{4,8},{8,12},{12,16},{16,20},{20,24},{24,28},{1,5},{5,9},{9,... | collective-permute-start | bytes 2888 | tf_op jit(solution)/shard_map/ppermute | solution.py:33
  170.6 7.0 %collective-permute-start.12 = (f32[3,8,10,1]{3,2,1,0:T(8,128)S(1)}, f32[3,8,10,1]{3,2,1,0:T(8,128)S(1)}, u32[]{:S(2)}, u32[]{:S(2)}) collective-permute-start(f32[3,8,10,1]{3,2,1,0:T(8,128)S(1)} %get-tuple-element.77), channel_id=1, source_target_pairs={{4,0},{8,4},{12,8},{16,12},{20,16},{24,20},{28,24},{5,1},{9,5},{13... | collective-permute-start | bytes 2888 | tf_op jit(solution)/shard_map/ppermute | solution.py:34
  177.7 4.9 %collective-permute-start.13 = (f32[3,1,10,130]{3,2,1,0:T(8,128)S(1)}, f32[3,1,10,130]{3,2,1,0:T(8,128)S(1)}, u32[]{:S(2)}, u32[]{:S(2)}) collective-permute-start(f32[3,1,10,130]{3,2,1,0:T(8,128)S(1)} %get-tuple-element.44), channel_id=1, source_target_pairs={{0,1},{1,2},{2,3},{4,5},{5,6},{6,7},{8,9},{9,10},{10,11},{12,13},{... | collective-permute-start | bytes 46808 | tf_op jit(solution)/shard_map/ppermute | solution.py:33
  180.4 4.8 %collective-permute-start.14 = (f32[3,1,10,130]{3,2,1,0:T(8,128)S(1)}, f32[3,1,10,130]{3,2,1,0:T(8,128)S(1)}, u32[]{:S(2)}, u32[]{:S(2)}) collective-permute-start(f32[3,1,10,130]{3,2,1,0:T(8,128)S(1)} %get-tuple-element.45), channel_id=1, source_target_pairs={{1,0},{2,1},{3,2},{5,4},{6,5},{7,6},{9,8},{10,9},{11,10},{13,12},{... | collective-permute-start | bytes 46808 | tf_op jit(solution)/shard_map/ppermute | solution.py:34
  188.6 15.3 %copy-start.5 = (f32[2,1,1,1024]{3,2,1,0:T(1,128)S(1)}, f32[2,1,1,1024]{3,2,1,0:T(1,128)}, u32[]{:S(2)}) copy-start(f32[2,1,1,1024]{3,2,1,0:T(1,128)} %param.23) | copy-start | bytes 24580
  188.7 5.2 %collective-permute-start.15 = (f32[3,8,1,128]{3,2,1,0:T(1,128)S(1)}, f32[3,8,1,128]{3,2,1,0:T(1,128)S(1)}, u32[]{:S(2)}, u32[]{:S(2)}) collective-permute-start(f32[3,8,1,128]{3,2,1,0:T(1,128)S(1)} %get-tuple-element.89), channel_id=1, source_target_pairs={{0,32},{32,64},{64,96},{96,128},{128,160},{160,192},{192,224},{224... | collective-permute-start | bytes 36872 | tf_op jit(solution)/shard_map/ppermute | solution.py:33
  192.6 4.4 %collective-permute-start.16 = (f32[3,8,1,128]{3,2,1,0:T(1,128)S(1)}, f32[3,8,1,128]{3,2,1,0:T(1,128)S(1)}, u32[]{:S(2)}, u32[]{:S(2)}) collective-permute-start(f32[3,8,1,128]{3,2,1,0:T(1,128)S(1)} %get-tuple-element.90), channel_id=1, source_target_pairs={{32,0},{64,32},{96,64},{128,96},{160,128},{192,160},{224,192},{256... | collective-permute-start | bytes 36872 | tf_op jit(solution)/shard_map/ppermute | solution.py:34
  197.2 7.4 %collective-permute-start.17 = (f32[3,8,10,1]{3,2,1,0:T(8,128)S(1)}, f32[3,8,10,1]{3,2,1,0:T(8,128)S(1)}, u32[]{:S(2)}, u32[]{:S(2)}) collective-permute-start(f32[3,8,10,1]{3,2,1,0:T(8,128)S(1)} %get-tuple-element.74), channel_id=1, source_target_pairs={{0,4},{4,8},{8,12},{12,16},{16,20},{20,24},{24,28},{1,5},{5,9},{9,... | collective-permute-start | bytes 2888 | tf_op jit(solution)/shard_map/ppermute | solution.py:33
  202.0 7.0 %collective-permute-start.18 = (f32[3,8,10,1]{3,2,1,0:T(8,128)S(1)}, f32[3,8,10,1]{3,2,1,0:T(8,128)S(1)}, u32[]{:S(2)}, u32[]{:S(2)}) collective-permute-start(f32[3,8,10,1]{3,2,1,0:T(8,128)S(1)} %get-tuple-element.75), channel_id=1, source_target_pairs={{4,0},{8,4},{12,8},{16,12},{20,16},{24,20},{28,24},{5,1},{9,5},{13... | collective-permute-start | bytes 2888 | tf_op jit(solution)/shard_map/ppermute | solution.py:34
  209.1 4.8 %collective-permute-start.19 = (f32[3,1,10,130]{3,2,1,0:T(8,128)S(1)}, f32[3,1,10,130]{3,2,1,0:T(8,128)S(1)}, u32[]{:S(2)}, u32[]{:S(2)}) collective-permute-start(f32[3,1,10,130]{3,2,1,0:T(8,128)S(1)} %get-tuple-element.40), channel_id=1, source_target_pairs={{0,1},{1,2},{2,3},{4,5},{5,6},{6,7},{8,9},{9,10},{10,11},{12,13},{... | collective-permute-start | bytes 46808 | tf_op jit(solution)/shard_map/ppermute | solution.py:33
  212.5 4.8 %collective-permute-start.20 = (f32[3,1,10,130]{3,2,1,0:T(8,128)S(1)}, f32[3,1,10,130]{3,2,1,0:T(8,128)S(1)}, u32[]{:S(2)}, u32[]{:S(2)}) collective-permute-start(f32[3,1,10,130]{3,2,1,0:T(8,128)S(1)} %get-tuple-element.41), channel_id=1, source_target_pairs={{1,0},{2,1},{3,2},{5,4},{6,5},{7,6},{9,8},{10,9},{11,10},{13,12},{... | collective-permute-start | bytes 46808 | tf_op jit(solution)/shard_map/ppermute | solution.py:34
  220.6 19.7 %copy-start.4 = (f32[3,8,8,128]{3,2,1,0:T(8,128)}, f32[3,8,8,128]{3,2,1,0:T(8,128)S(1)}, u32[]{:S(2)}) copy-start(f32[3,8,8,128]{3,2,1,0:T(8,128)S(1)} %fusion.34) | copy-start | bytes 294916
  253.2 10.8 %collective-permute-start.23 = (f32[256,128]{1,0:T(8,128)S(1)}, f32[256,128]{1,0:T(8,128)S(1)}, u32[]{:S(2)}, u32[]{:S(2)}) collective-permute-start(f32[256,128]{1,0:T(8,128)S(1)} %bitcast.153), channel_id=1, source_target_pairs={{0,32},{32,64},{64,96},{96,128},{128,160},{160,192},{192,224},{224... | collective-permute-start | bytes 393224 | tf_op jit(solution)/shard_map/ppermute | solution.py:42
  254.9 11.4 %collective-permute-start.21 = (f32[256,128]{1,0:T(8,128)S(1)}, f32[256,128]{1,0:T(8,128)S(1)}, u32[]{:S(2)}, u32[]{:S(2)}) collective-permute-start(f32[256,128]{1,0:T(8,128)S(1)} %bitcast.152), channel_id=1, source_target_pairs={{0,4},{4,8},{8,12},{12,16},{16,20},{20,24},{24,28},{1,5},{5,9},{9,... | collective-permute-start | bytes 393224 | tf_op jit(solution)/shard_map/ppermute | solution.py:42
  260.4 5.9 %collective-permute-start.22 = (f32[256,128]{1,0:T(8,128)S(1)}, f32[256,128]{1,0:T(8,128)S(1)}, u32[]{:S(2)}, u32[]{:S(2)}) collective-permute-start(f32[256,128]{1,0:T(8,128)S(1)} %bitcast.151), channel_id=1, source_target_pairs={{0,32},{32,64},{64,96},{96,128},{128,160},{160,192},{192,224},{224... | collective-permute-start | bytes 393224 | tf_op jit(solution)/shard_map/ppermute | solution.py:42
  264.0 4.1 %collective-permute-start.24 = (f32[256,128]{1,0:T(8,128)S(1)}, f32[256,128]{1,0:T(8,128)S(1)}, u32[]{:S(2)}, u32[]{:S(2)}) collective-permute-start(f32[256,128]{1,0:T(8,128)S(1)} %collective-permute-done.23), channel_id=1, source_target_pairs={{0,4},{4,8},{8,12},{12,16},{16,20},{20,24},{24,28},{1,5},{5,9},{9,... | collective-permute-start | bytes 393224 | tf_op jit(solution)/shard_map/ppermute | solution.py:42
where the time goes:
time: 271 us; the launch traced here: 269 us
  blocking collectives  117 us (43%)
  starting transfers between devices  73.2 us (27%)
  other arithmetic  37.1 us (14%)
  waiting for transfers between devices  35.6 us (13%)
  between operations  3.63 us (1%)
    pmax x1, blocking collectives, per_device(): top_bound = lax.pmax(local_bound, ('gx', 'gy', 'gz'))  110 us
    ppermute x9, starting transfers between devices, padded_2(): before = lax.ppermute(last, axis, up)  34 us
    ppermute x9, waiting for transfers between devices, padded_2(): after = lax.ppermute(first, axis, down)  28.9 us
    ppermute x7, starting transfers between devices, passed_along(): return lax.ppermute(block, axis, route)  23.8 us
    ppermute x9, starting transfers between devices, padded_2(): after = lax.ppermute(first, axis, down)  15.5 us
    psum x1, blocking collectives, per_device(): column = lax.psum(column, 'gz')  7.27 us
    scatter-add x1, other arithmetic, per_device(): elevation_grid.at[flattened_location + 1].add(weighted_contribution[1])  6.27 us
    scatter-add x1, other arithmetic, per_device(): elevation_grid.at[flattened_location + 2 * TILE_COLUMNS]  6.27 us
  transfers between devices with their start and end apart: 25, of which 13 were waited for; matrix products, arithmetic and copies ran while one was open for 0% of the time, Pallas kernels for 0%

commit v1 on v0

v1 whole, which is shorter than its diff:
```python
import functools
import itertools

import jax
import jax.numpy as jnp
from jax import lax
from jax.experimental import pallas as pl
from jax.experimental.pallas import tpu as pltpu
from jax.sharding import PartitionSpec as P

MESH = pl.DeviceIdType.MESH
F32, BF16 = jnp.float32, jnp.bfloat16
NX, NY, NZ = 16, 8, 4
BZ, BX, BY = 8, 8, 128
TILE_ROWS, TILE_COLUMNS = 256, 128
VARIABLES = 6
SZ, WZ, AZ = 13, 11, 9
EDGE_Z, INNER_Z = (5, 6, 7, 0, 1), (2, 3, 4)

NEAR = [d for d in itertools.product((-1, 0, 1), repeat=3) if d != (0, 0, 0)]
PLANE = sorted(
    [(b, c) for b in range(NY) for c in range(NZ) if (b, c) != (0, 0)],
    key=lambda d: -(min(d[0], NY - d[0]) // 2 + min(d[1], NZ - d[1])),
)
GROUND = [(a, b, c) for a in (0, 1) for b in (0, 1) for c in range(NZ)]


def near_index(d):
    return (d[0] + 1) * 9 + (d[1] + 1) * 3 + d[2] + 1


def guarded(condition, act):
    if condition is None:
        act()
    else:
        pl.when(condition)(act)


def rows_between(dx):
    if dx == 0:
        return pl.ds(0, 8), pl.ds(0, 8)
    return (pl.ds(4, 4), pl.ds(12, 4)) if dx == 1 else (pl.ds(0, 4), pl.ds(8, 4))


def layers_between(dz, below, above):
    if dz == 0:
        return pl.ds(0, BZ), pl.ds(below, BZ)
    if dz == 1:
        return pl.ds(BZ - below, below), pl.ds(0, below)
    return pl.ds(0, above), pl.ds(below + BZ, above)


def kernel(
    adj_h, lin_h, stiff_h, anchor_h, tile_h, row_h, col_h, off_h,
    def_o, dem_o,
    adj_v, lin_v, stiff_v, anchor_v, tile_v, row_v, col_v, off_v,
    AX, PA, PAE, WX, PW, PWE, EX, PS, PSE, TE, W16, DG, G, K1, K2, CE, P1, P2, P3,
    RH, RL, CV,
    load_sem, w_send, w_recv, a_send, a_recv, t_send, t_recv, s_send, s_recv,
    e_send, e_recv, p1_send, p1_recv, p2_send, p2_recv, p3_send, p3_recv,
):
    gx, gy, gz = lax.axis_index("gx"), lax.axis_index("gy"), lax.axis_index("gz")

    def at(dx, dy, dz):
        return (gx + dx, lax.rem(gy + dy + NY, NY), lax.rem(gz + dz + NZ, NZ))

    first, last = gx == 0, gx == NX - 1
    not_first, not_last = gx > 0, gx < NX - 1
    can_send = {0: None, 1: not_last, -1: not_first}
    can_receive = {0: None, 1: not_first, -1: not_last}

    barrier = pltpu.get_barrier_semaphore()

    def greet(device):
        pl.semaphore_signal(barrier, inc=1, device_id=device, device_id_type=MESH)

    def greet_x(dx):
        for dy in (-1, 0, 1):
            for dz in (-1, 0, 1):
                greet(at(dx, dy, dz))

    for b, c in PLANE:
        greet(at(0, b, c))
    pl.when(not_first)(functools.partial(greet_x, -1))
    pl.when(not_last)(functools.partial(greet_x, 1))

    @pl.when(first)
    def _():
        for i in range(1, NX):
            greet((i, gy, gz))

    loads = [
        pltpu.make_async_copy(h, v, load_sem.at[i])
        for i, (h, v) in enumerate(
            ((stiff_h, stiff_v), (anchor_h, anchor_v), (adj_h, adj_v), (tile_h, tile_v),
             (row_h, row_v), (col_h, col_v), (off_h, off_v), (lin_h, lin_v))
        )
    ]
    for copy in loads:
        copy.start()

    lane = lax.broadcasted_iota(jnp.int32, (8, 128), 1)

    loads[0].wait()
    loads[1].wait()
    packed = jnp.zeros((8, 128), F32)
    for f, source in enumerate((stiff_v, anchor_v)):
        values = source[...].astype(F32)
        WX[f, 2:10, 0:8, 0:128] = values
        for z in range(BZ):
            w = f * BZ + z
            packed = jnp.where(lane // 8 == w, pltpu.roll(values[z], (8 * w + 4) % 128, 1), packed)
    PW[...] = packed

    loads[2].wait()
    packed = jnp.zeros((8, 128), F32)
    for v in range(VARIABLES):
        values = adj_v[v].astype(F32)
        AX[v, 0:8, 0:8, 0:128] = values
        for z in range(BZ):
            w = v * BZ + z
            packed = jnp.where(lane == w, pltpu.roll(values[z], w, 1), packed)
    PA[...] = packed

    for i in range(3, 7):
        loads[i].wait()
    TE[0, 0] = tile_v[...].astype(F32)
    TE[0, 1] = row_v[...].astype(F32)
    TE[0, 2] = col_v[...].astype(F32)
    TE[0, 3] = off_v[0]
    TE[0, 4] = off_v[1]

    pl.semaphore_wait(
        barrier,
        len(PLANE) + jnp.where(not_first, 10, 0) + jnp.where(not_last, 9, 0),
    )

    def w_copy(d):
        dx, dy, dz = d
        rs, rd = rows_between(dx)
        if dy == 0:
            zs, zd = layers_between(dz, 2, 1)
            src, dst = WX.at[:, pl.ds(2 + zs.start, zs.size), rs, 0:128], WX.at[:, zd, rs_at(rd), 0:128]
        else:
            src, dst = PW.at[rs], PWE.at[0 if dy == 1 else 1, 1 - dz, rd]
        i = near_index(d)
        return pltpu.make_async_remote_copy(
            src, dst, w_send.at[i], w_recv.at[i], device_id=at(*d), device_id_type=MESH
        )

    def rs_at(rd):
        return rd

    def a_copy(d):
        dx, dy, dz = d
        rs, rd = (pl.ds(0, 8), pl.ds(0, 8)) if dx == 0 else (pl.ds(0, 1), pl.ds(8, 1))
        if dy == 0:
            zs, zd = (pl.ds(0, 8), pl.ds(0, 8)) if dz == 0 else (pl.ds(0, 1), pl.ds(8, 1))
            src, dst = AX.at[:, zs, rs, 0:128], AX.at[:, zd, rd, 0:128]
        else:
            src, dst = PA.at[rs], PAE.at[-dz, rd]
        i = near_index(d)
        return pltpu.make_async_remote_copy(
            src, dst, a_send.at[i], a_recv.at[i], device_id=at(*d), device_id_type=MESH
        )

    def t_copy(a, b):
        i = 2 * a + b
        return pltpu.make_async_remote_copy(
            TE.at[0], TE.at[i], t_send.at[i], t_recv.at[i], device_id=at(a, b, 0), device_id_type=MESH
        )

    w_copies = [(d[0], w_copy(d)) for d in sorted(NEAR, key=lambda d: -sum(x >= 0 for x in d))]
    a_copies = [(d[0], a_copy(d)) for d in NEAR if max(d) <= 0]
    t_copies = [(a, t_copy(a, b)) for a, b in ((0, 1), (1, 0), (1, 1))]

    def start_all(copies):
        for step in (0, 1, -1):
            these = [c for dx, c in copies if dx == step]

            def go(these=these):
                for c in these:
                    c.start()

            guarded(can_send[step], go)

    def receive_all(copies):
        for step in (0, 1, -1):
            these = [c for dx, c in copies if dx == step]

            def go(these=these):
                for c in these:
                    c.wait_recv()

            guarded(can_receive[step], go)

    def sent_all(copies):
        for step in (0, 1, -1):
            these = [c for dx, c in copies if dx == step]

            def go(these=these):
                for c in these:
                    c.wait_send()

            guarded(can_send[step], go)

    start_all(w_copies)
    start_all(a_copies)
    start_all(t_copies)

    row16 = lax.broadcasted_iota(jnp.int32, (16, 256), 0)
    lane256 = lax.broadcasted_iota(jnp.int32, (16, 256), 1)
    ex = gx * BX + jnp.where(row16 < 12, row16, row16 - 16)
    ey = gy * BY + jnp.where(lane256 < 192, lane256, lane256 - 256)
    node_xy = (ex >= 0) & (ex <= NX * BX - 1) & (ey >= 0) & (ey <= NY * BY - 1)
    element_xy = (ex >= 0) & (ex <= NX * BX - 2) & (ey >= 0) & (ey <= NY * BY - 2)

    def node_mask(z):
        ez = gz * BZ + z
        return node_xy & (ez >= 0) & (ez <= NZ * BZ - 1)

    def element_mask(z):
        ez = gz * BZ + z
        return element_xy & (ez >= 0) & (ez <= NZ * BZ - 2)

    window16 = lax.broadcasted_iota(jnp.int32, (16, 128), 1)
    from_left = lax.rem(window16, 8) < 4

    receive_all(w_copies)
    for f in range(2):
        for z in range(-2, 9):
            slot, zz = (0, z + 8) if z < 0 else (1, z) if z < 8 else (2, z - 8)
            mixed = jnp.where(from_left, PWE[0, slot], PWE[1, slot])
            w = f * BZ + zz
            WX[f, z + 2, :, 128:256] = pltpu.roll(mixed, (124 - 8 * w) % 128, 1)
    for z in range(-2, 9):
        W16[z + 2] = jnp.where(element_mask(z), WX[0, z + 2], 0.0) * (1.0 / 16.0)
    highest = jnp.zeros((8, 128), F32)
    for z in range(-1, 9):
        total = W16[z + 1] + W16[z + 2]
        total = total + pltpu.roll(total, 1, 0)
        total = total + pltpu.roll(total, 1, 1)
        spring = jnp.where(node_mask(z), WX[1, z + 2], 0.0)
        DG[z + 1] = spring + 4.0 * total
        if 0 <= z < 8:
            highest = jnp.maximum(highest, (spring + 44.0 * total)[0:8, 0:128])

    P1[0:1] = jnp.max(highest, axis=0, keepdims=True)
    for b, c in PLANE:
        i = b * NZ + c
        pltpu.make_async_remote_copy(
            P1.at[pl.ds(0, 1)], P1.at[pl.ds(i, 1)], p1_send, p1_recv, device_id=at(0, b, c), device_id_type=MESH
        ).start()

    receive_all(a_copies)
    loads[7].wait()
    averages = []
    for v in range(VARIABLES):
        layers = []
        for z in range(BZ + 1):
            slot, zz = (0, z) if z < 8 else (1, 0)
            side = pltpu.roll(PAE[slot], (128 - (v * BZ + zz)) % 128, 1)
            layers.append(jnp.concatenate([AX[v, z, :, 0:128], side], axis=1))
        for z in range(BZ):
            total = layers[z] + layers[z + 1]
            total = total + pltpu.roll(total, 15, 0)
            total = total[0:8]
            total = total + pltpu.roll(total, 255, 1)
            AX[v, z, 0:8, 128:256] = total[:, 0:128] * (0.125 * 0.25)
    packs = [jnp.zeros((8, 128), F32), jnp.zeros((8, 128), F32)]
    for c in range(3):
        for z in range(BZ):
            total = lin_v[c, z].astype(F32) * AX[0, z, 0:8, 128:256]
            for v in range(1, VARIABLES):
                total = total + lin_v[3 * v + c, z].astype(F32) * AX[v, z, 0:8, 128:256]
            EX[c, z + 3, 0:8, 0:128] = total
            if z in EDGE_Z:
                t, w = 0, c * 5 + EDGE_Z.index(z)
            else:
                t, w = 1, c * 3 + INNER_Z.index(z)
            packs[t] = jnp.where(lane // 8 == w, pltpu.roll(total, (8 * w + 4) % 128, 1), packs[t])
    PS[0] = packs[0]
    PS[1] = packs[1]

    def s_copy(d):
        dx, dy, dz = d
        rs, rd = rows_between(dx)
        if dy == 0:
            zs, zd = layers_between(dz, 3, 2)
            src = EX.at[:, pl.ds(3 + zs.start, zs.size), rs, 0:128]
            dst = EX.at[:, zd, rd, 0:128]
        else:
            side = 0 if dy == 1 else 1
            if dz == 0:
                src, dst = PS.at[:, rs], PSE.at[side, pl.ds(1, 2), rd]
            else:
                src, dst = PS.at[0, rs], PSE.at[side, 0 if dz == 1 else 3, rd]
        i = near_index(d)
        return pltpu.make_async_remote_copy(
            src, dst, s_send.at[i], s_recv.at[i], device_id=at(*d), device_id_type=MESH
        )

    s_copies = [(d[0], s_copy(d)) for d in sorted(NEAR, key=lambda d: abs(d[1]))]
    start_all(s_copies)

    receive_all(t_copies)
    mine = (gx * NY + gy).astype(F32)
    rows = lax.broadcasted_iota(jnp.int32, (256, 128), 0).astype(F32)
    columns = lax.broadcasted_iota(jnp.int32, (128, 128), 0).astype(F32)
    for q in range(4):
        here = TE[q, 0] == mine
        if q >= 2:
            here = here & not_first
        row_at = jnp.where(here, TE[q, 1], -9.0)
        col_at = jnp.where(here, TE[q, 2], -9.0)
        fr = jnp.where(here, TE[q, 3], 0.0)
        fc = jnp.where(here, TE[q, 4], 0.0)
        for x in range(BX):
            part = pl.ds((q * BX + x) * 128, 128)
            r, f = row_at[x : x + 1], fr[x : x + 1]
            value = jnp.where(rows == r, 1.0 - f, jnp.where(rows == r + 1.0, f, 0.0))
            high = value.astype(BF16)
            RH[:, part] = high
            RL[:, part] = (value - high.astype(F32)).astype(BF16)
            r, f = col_at[x : x + 1], fc[x : x + 1]
            CV[:, part] = jnp.where(columns == r, 1.0 - f, jnp.where(columns == r + 1.0, f, 0.0))

    pltpu.make_async_copy(P1.at[pl.ds(1, 31)], P1.at[pl.ds(1, 31)], p1_recv).wait()
    plane_highest = jnp.max(P1[...], axis=0, keepdims=True)
    P2[0:1] = plane_highest
    up = pltpu.make_async_remote_copy(
        P2.at[pl.ds(0, 1)], P2.at[pl.ds(gx, 1)], p2_send, p2_recv, device_id=(0, gy, gz), device_id_type=MESH
    )
    pl.when(not_first)(up.start)

    receive_all(s_copies)
    for side_slot in range(1):
        mixed = [jnp.where(from_left, PSE[0, s], PSE[1, s]) for s in range(4)]
        for c in range(3):
            for z in range(-3, 10):
                zz = z % 8
                if zz in EDGE_Z:
                    slot, w = (0 if z < 0 else 3 if z >= 8 else 1), c * 5 + EDGE_Z.index(zz)
                else:
                    slot, w = 2, c * 3 + INNER_Z.index(zz)
                EX[c, z + 3, :, 128:256] = pltpu.roll(mixed[slot], (124 - 8 * w) % 128, 1)

    def ahead_x(value):
        return pltpu.roll(value, 15, 0)

    def ahead_y(value):
        return pltpu.roll(value, 255, 1)

    def behind_x(value):
        return pltpu.roll(value, 1, 0)

    def behind_y(value):
        return pltpu.roll(value, 1, 1)

    held = None
    for z in range(-3, 10):
        mask = element_mask(z)
        sense = [jnp.where(mask, EX[c, z + 3], 0.0) for c in range(3)]
        if held is not None:
            qx, qy, qz = held[0] + sense[0], held[1] + sense[1], held[2] - sense[2]
            qx, qy, qz = behind_x(qx) - qx, behind_x(qy) + qy, behind_x(qz) + qz
            G[0, z + 2] = behind_y(qx) + qx
            G[1, z + 2] = behind_y(qy) - qy
            G[2, z + 2] = behind_y(qz) + qz
        held = sense

    def element_forces(low, high, weight):
        gradient, middle = [], []
        for c in range(3):
            a, b = high[c] + low[c], high[c] - low[c]
            a1, b1 = ahead_y(a), ahead_y(b)
            sy, dy, sz = a1 + a, a1 - a, b1 + b
            sy1, dy1, sz1 = ahead_x(sy), ahead_x(dy), ahead_x(sz)
            middle.append(sy1 + sy)
            gradient.append((sy1 - sy, dy1 + dy, sz1 + sz))
        trace = gradient[0][0] + gradient[1][1] + gradient[2][2]
        half = 0.5 * weight
        plus, minus = [], []
        for c in range(3):
            s = [
                weight * (2.0 * gradient[c][c] + trace if c == d else gradient[c][d] + gradient[d][c])
                for d in range(3)
            ]
            m = half * middle[c]
            q = behind_x(s[0] - m) - (s[0] + m)
            q2 = behind_x(s[1]) + s[1]
            q3 = behind_x(s[2]) + s[2]
            r1 = behind_y(q + q2) + (q - q2)
            r2 = behind_y(q3) + q3
            plus.append(r1 + r2)
            minus.append(r1 - r2)
        return plus, minus

    held = None
    for j in range(11):
        plus, minus = element_forces([G[c, j] for c in range(3)], [G[c, j + 1] for c in range(3)], W16[j])
        if held is not None:
            for c in range(3):
                K1[c, j - 1] = held[c] + minus[c] + DG[j - 1] * G[c, j]
        held = plus

    sums = [jnp.zeros((8, 128), F32) for _ in range(3)]
    held = None
    for j in range(9):
        plus, minus = element_forces([K1[c, j] for c in range(3)], [K1[c, j + 1] for c in range(3)], W16[j + 1])
        if held is not None:
            z = j - 1
            for c in range(3):
                value = held[c] + minus[c] + DG[j] * K1[c, j]
                K2[c, z] = value[0:8, 0:128]
            share = ((NZ * BZ - 1 - z) - gz * BZ).astype(F32) * (1.0 / (NZ * BZ - 1))
            sums[0] = sums[0] + share * G[2, z + 2, 0:8, 0:128]
            sums[1] = sums[1] + share * K1[2, z + 1, 0:8, 0:128]
            sums[2] = sums[2] + share * K2[2, z]
        held = plus
    for k in range(3):
        CE[0, k] = sums[k]

    def e_copy(a, b, c):
        i = a * 8 + b * 4 + c
        return pltpu.make_async_remote_copy(
            CE.at[0], CE.at[i], e_send.at[a], e_recv.at[a], device_id=at(a, b, c), device_id_type=MESH
        )

    for a in (0, 1):
        these = [e_copy(*d) for d in GROUND if d[0] == a and d != (0, 0, 0)]

        def go(these=these):
            for copy in these:
                copy.start()

        guarded(can_send[a], go)

    @pl.when(first)
    def _():
        pltpu.make_async_copy(P2.at[pl.ds(1, 15)], P2.at[pl.ds(1, 15)], p2_recv).wait()
        P3[...] = jnp.max(P2[...], axis=0, keepdims=True)
        for i in range(1, NX):
            pltpu.make_async_remote_copy(
                P3, P3, p3_send, p3_recv, device_id=(i, gy, gz), device_id_type=MESH
            ).start()

    @pl.when(not_first)
    def _():
        pltpu.make_async_copy(P3, P3, p3_recv).wait()

    top = jnp.max(P3[...], axis=1, keepdims=True)
    low = top / 30.0
    center = 0.5 * (top + low)
    half_width = 0.5 * (top - low)
    ratio = center / half_width
    rho0 = 1.0 / ratio
    rho1 = 1.0 / (2.0 * ratio - rho0)
    rho2 = 1.0 / (2.0 * ratio - rho1)
    inverse = 1.0 / center
    a1, b1 = rho1 * rho0, 2.0 * rho1 / half_width
    a2, b2 = rho2 * rho1, 2.0 * rho2 / half_width
    p, q = a1 * inverse + b1, -b1 * inverse
    k0 = inverse + p + a2 * p + b2
    k1 = q + a2 * q - b2 * (inverse + p)
    k2 = -b2 * q
    k0, k1, k2 = [jnp.broadcast_to(k, (8, 128)) for k in (k0, k1, k2)]
    for c in range(3):
        for z in range(BZ):
            def_o[c, z] = k0 * G[c, z + 2, 0:8, 0:128] + k1 * K1[c, z + 1, 0:8, 0:128] + k2 * K2[c, z]

    pltpu.make_async_copy(CE.at[pl.ds(1, 7)], CE.at[pl.ds(1, 7)], e_recv.at[0]).wait()

    @pl.when(not_first)
    def _():
        pltpu.make_async_copy(CE.at[pl.ds(8, 8)], CE.at[pl.ds(8, 8)], e_recv.at[1]).wait()

    result = jnp.zeros((256, 128), F32)
    for q in range(4):
        parts = [
            CE[4 * q, k] + CE[4 * q + 1, k] + CE[4 * q + 2, k] + CE[4 * q + 3, k] for k in range(3)
        ]
        column = k0 * parts[0] + k1 * parts[1] + k2 * parts[2]
        if q >= 2:
            column = jnp.where(not_first, column, 0.0)
        for x in range(BX):
            part = pl.ds((q * BX + x) * 128, 128)
            value = CV[:, part] * column[x : x + 1]
            high = value.astype(BF16)
            rest = (value - high.astype(F32)).astype(BF16)
            both = jnp.concatenate([high, rest], axis=0)
            dims = (((1,), (1,)), ((), ()))
            pair = lax.dot_general(RH[:, part], both, dims, preferred_element_type=F32)
            result = result + pair[:, 0:128] + pair[:, 128:256]
            result = result + lax.dot_general(RL[:, part], high, dims, preferred_element_type=F32)
    dem_o[...] = result

    sent_all(w_copies)
    sent_all(a_copies)
    sent_all(t_copies)
    sent_all(s_copies)
    pltpu.make_async_copy(P1.at[pl.ds(1, 31)], P1.at[pl.ds(1, 31)], p1_send).wait()
    pl.when(not_first)(up.wait_send)
    pltpu.make_async_copy(CE.at[pl.ds(1, 7)], CE.at[pl.ds(1, 7)], e_send.at[0]).wait()

    @pl.when(not_last)
    def _():
        pltpu.make_async_copy(CE.at[pl.ds(8, 8)], CE.at[pl.ds(8, 8)], e_send.at[1]).wait()

    @pl.when(first)
    def _():
        pltpu.make_async_copy(P2.at[pl.ds(1, 15)], P2.at[pl.ds(1, 15)], p3_send).wait()


def per_device(adjoint, linearized, stiffness, anchor, target_tile, target_row, target_col, offsets):
    vmem = lambda *shape, dtype=F32: pltpu.VMEM(shape, dtype)
    dma = pltpu.SemaphoreType.DMA
    ground = (BX, BY)
    return pl.pallas_call(
        kernel,
        out_shape=(
            jax.ShapeDtypeStruct((3, BZ, BX, BY), F32),
            jax.ShapeDtypeStruct((TILE_ROWS, TILE_COLUMNS), F32),
        ),
        in_specs=[pl.BlockSpec(memory_space=pl.ANY)] * 8,
        out_specs=[pl.BlockSpec(memory_space=pltpu.VMEM)] * 2,
        scratch_shapes=[
            vmem(6, BZ, BX, BY, dtype=BF16), vmem(18, BZ, BX, BY, dtype=BF16),
            vmem(BZ, BX, BY, dtype=BF16), vmem(BZ, BX, BY),
            vmem(*ground, dtype=jnp.int32), vmem(*ground, dtype=jnp.int32),
            vmem(*ground, dtype=jnp.int32), vmem(2, *ground),
            vmem(VARIABLES, AZ, 16, 256), vmem(8, 128), vmem(2, 16, 128),
            vmem(2, WZ, 16, 256), vmem(8, 128), vmem(2, 3, 16, 128),
            vmem(3, SZ, 16, 256), vmem(2, 8, 128), vmem(2, 4, 16, 128),
            vmem(4, 5, 8, 128),
            vmem(WZ, 16, 256), vmem(10, 16, 256),
            vmem(3, 12, 16, 256), vmem(3, 10, 16, 256), vmem(3, BZ, BX, BY),
            vmem(16, 3, 8, 128), vmem(32, 128), vmem(16, 128), vmem(1, 128),
            vmem(256, 4096, dtype=BF16), vmem(256, 4096, dtype=BF16), vmem(128, 4096),
            dma((8,)), dma((27,)), dma((27,)), dma((27,)), dma((27,)), dma((4,)), dma((4,)),
            dma((27,)), dma((27,)), dma((2,)), dma((2,)), dma, dma, dma, dma, dma, dma,
        ],
        compiler_params=pltpu.CompilerParams(
            collective_id=0, has_side_effects=True, vmem_limit_bytes=48 * 1024 * 1024
        ),
    )(
        adjoint, linearized, stiffness, anchor,
        target_tile.reshape(ground), target_row.reshape(ground), target_col.reshape(ground),
        offsets.reshape((2,) + ground),
    )


def solution(mesh):
    in_specs = (
        P(None, "gz", "gx", "gy"),
        P(None, "gz", "gx", "gy"),
        P("gz", "gx", "gy"),
        P("gz", "gx", "gy"),
        P("gx", "gy", None, None),
        P("gx", "gy", None),
        P("gx", "gy", None),
        P(None, "gx", "gy", None),
    )
    out_specs = (P(None, "gz", "gx", "gy"), P("gy", "gx"))
    return jax.shard_map(per_device, mesh=mesh, in_specs=in_specs, out_specs=out_specs, check_vma=False)
```

time: 271 us -> 45.6 us (0.17)
  the two profiles are of different devices: /device:TPU:1 before, /device:TPU:32 now
where the time goes in v1:
time: 45.6 us; the launch traced here: 45.2 us
  Pallas kernels  37.1 us (81%)
  local copies, waits for them, and re-layouts  7.37 us (16%)
  between operations  0.66 us (1%)
    pallas_call x1, Pallas kernels, per_device(): pl.pallas_call(kernel, out_shape=(jax.ShapeDtypeStruct((3, BZ, BX, BY), F...  37.1 us
    unnamed x18, local copies, waits for them, and re-layouts  7.37 us

profile of v1, /device:TPU:32, one launch (start us, length us, event | category | flops | bytes accessed | tf_op | source)
XLA Modules:
  0.0 45.2 jit_solution(18097420202238966002)
XLA Ops:
  0.6 0.0 copy-start.5
  0.6 0.7 %copy-done.5 = s32[1,1,1024,1]{2,3,1,0:T(1,128)S(1)} copy-done((s32[1,1,1024,1]{2,3,1,0:T(1,128)S(1)}, s32[1,1,1024,1]{2,3,1,0:T(1,128)}, u32[]{:S(2)}) %copy-start.5) | copy-done | bytes 4120
  1.3 0.0 copy-start
  1.3 1.0 %copy-done = bf16[18,8,8,128]{3,2,1,0:T(8,128)(2,1)S(1)} copy-done((bf16[18,8,8,128]{3,2,1,0:T(8,128)(2,1)S(1)}, bf16[18,8,8,128]{3,2,1,0:T(8,128)(2,1)}, u32[]{:S(2)}) %copy-start) | copy-done | bytes 294936
  2.3 0.0 copy-start.1
  2.3 0.9 %copy-done.1 = bf16[6,8,8,128]{3,2,1,0:T(8,128)(2,1)S(1)} copy-done((bf16[6,8,8,128]{3,2,1,0:T(8,128)(2,1)S(1)}, bf16[6,8,8,128]{3,2,1,0:T(8,128)(2,1)}, u32[]{:S(2)}) %copy-start.1) | copy-done | bytes 98328
  3.2 0.0 copy-start.2
  3.2 0.8 %copy-done.2 = f32[8,8,128]{2,1,0:T(8,128)S(1)} copy-done((f32[8,8,128]{2,1,0:T(8,128)S(1)}, f32[8,8,128]{2,1,0:T(8,128)}, u32[]{:S(2)}) %copy-start.2) | copy-done | bytes 32792
  3.9 0.0 copy-start.3
  3.9 0.7 %copy-done.3 = bf16[8,8,128]{2,1,0:T(8,128)(2,1)S(1)} copy-done((bf16[8,8,128]{2,1,0:T(8,128)(2,1)S(1)}, bf16[8,8,128]{2,1,0:T(8,128)(2,1)}, u32[]{:S(2)}) %copy-start.3) | copy-done | bytes 16408
  4.7 0.0 copy-start.4
  4.7 0.7 %copy-done.4 = f32[2,1,1,1024]{3,2,1,0:T(1,128)S(1)} copy-done((f32[2,1,1,1024]{3,2,1,0:T(1,128)S(1)}, f32[2,1,1,1024]{3,2,1,0:T(1,128)}, u32[]{:S(2)}) %copy-start.4) | copy-done | bytes 8216
  5.3 0.0 copy-start.6
  5.4 0.7 %copy-done.6 = s32[1,1,1024]{2,1,0:T(1,128)S(1)} copy-done((s32[1,1,1024]{2,1,0:T(1,128)S(1)}, s32[1,1,1024]{2,1,0:T(1,128)}, u32[]{:S(2)}) %copy-start.6) | copy-done | bytes 4120
  6.0 0.0 copy-start.7
  6.0 0.7 %copy-done.7 = s32[1,1,1024]{2,1,0:T(1,128)S(1)} copy-done((s32[1,1,1024]{2,1,0:T(1,128)S(1)}, s32[1,1,1024]{2,1,0:T(1,128)}, u32[]{:S(2)}) %copy-start.7) | copy-done | bytes 4120
  6.7 37.1 %shard_map.95 = (f32[3,8,8,128]{3,2,1,0:T(8,128)S(1)}, f32[256,128]{1,0:T(8,128)S(1)}) custom-call(bf16[6,8,8,128]{3,2,1,0:T(8,128)(2,1)S(1)} %copy-done.1, bf16[18,8,8,128]{3,2,1,0:T(8,128)(2,1)S(1)} %copy-done, bf16[8,8,128]{2,1,0:T(8,128)(2,1)S(1)} %copy-done.3, f32[8,8,128]{2,1,0:T(8,128)S(1)} %copy-done.2, s32[8,128]{1,0:T(8,128)S(1)} %bitcast.5, ...), custom_call_target="tpu_custom_call" | custom-call | tf_op jit(solution)/shard_map/pallas_call | solution.py:519
  43.9 0.6 %copy.12 = f32[3,8,8,128]{3,2,1,0:T(8,128)} copy(f32[3,8,8,128]{3,2,1,0:T(8,128)S(1)} %get-tuple-element.4) | data formatting | bytes 196608
  44.5 0.7 %copy.13 = f32[256,128]{1,0:T(8,128)} copy(f32[256,128]{1,0:T(8,128)S(1)} %get-tuple-element.5) | data formatting | bytes 262144
Async XLA Ops:
  0.6 0.7 %copy-start.5 = (s32[1,1,1024,1]{2,3,1,0:T(1,128)S(1)}, s32[1,1,1024,1]{2,3,1,0:T(1,128)}, u32[]{:S(2)}) copy-start(s32[1,1,1024,1]{2,3,1,0:T(1,128)} %param.12) | copy-start | bytes 12292
  1.3 1.0 %copy-start = (bf16[18,8,8,128]{3,2,1,0:T(8,128)(2,1)S(1)}, bf16[18,8,8,128]{3,2,1,0:T(8,128)(2,1)}, u32[]{:S(2)}) copy-start(bf16[18,8,8,128]{3,2,1,0:T(8,128)(2,1)} %lin_h.1) | copy-start | bytes 884740
  2.3 0.9 %copy-start.1 = (bf16[6,8,8,128]{3,2,1,0:T(8,128)(2,1)S(1)}, bf16[6,8,8,128]{3,2,1,0:T(8,128)(2,1)}, u32[]{:S(2)}) copy-start(bf16[6,8,8,128]{3,2,1,0:T(8,128)(2,1)} %adj_h.1) | copy-start | bytes 294916
  3.2 0.8 %copy-start.2 = (f32[8,8,128]{2,1,0:T(8,128)S(1)}, f32[8,8,128]{2,1,0:T(8,128)}, u32[]{:S(2)}) copy-start(f32[8,8,128]{2,1,0:T(8,128)} %anchor_h.1) | copy-start | bytes 98308
  3.9 0.7 %copy-start.3 = (bf16[8,8,128]{2,1,0:T(8,128)(2,1)S(1)}, bf16[8,8,128]{2,1,0:T(8,128)(2,1)}, u32[]{:S(2)}) copy-start(bf16[8,8,128]{2,1,0:T(8,128)(2,1)} %stiff_h.1) | copy-start | bytes 49156
  4.7 0.7 %copy-start.4 = (f32[2,1,1,1024]{3,2,1,0:T(1,128)S(1)}, f32[2,1,1,1024]{3,2,1,0:T(1,128)}, u32[]{:S(2)}) copy-start(f32[2,1,1,1024]{3,2,1,0:T(1,128)} %param.15) | copy-start | bytes 24580
  5.3 0.7 %copy-start.6 = (s32[1,1,1024]{2,1,0:T(1,128)S(1)}, s32[1,1,1024]{2,1,0:T(1,128)}, u32[]{:S(2)}) copy-start(s32[1,1,1024]{2,1,0:T(1,128)} %param.13) | copy-start | bytes 12292
  6.0 0.7 %copy-start.7 = (s32[1,1,1024]{2,1,0:T(1,128)S(1)}, s32[1,1,1024]{2,1,0:T(1,128)}, u32[]{:S(2)}) copy-start(s32[1,1,1024]{2,1,0:T(1,128)} %param.14) | copy-start | bytes 12292

commit v2 on v1

--- a/solution.py
+++ b/solution.py
@@ -22,6 +22,10 @@
     [(b, c) for b in range(NY) for c in range(NZ) if (b, c) != (0, 0)],
     key=lambda d: -(min(d[0], NY - d[0]) // 2 + min(d[1], NZ - d[1])),
 )
+DOWN = [d for d in NEAR if max(d) <= 0]
+UP = [d for d in NEAR if min(d) >= 0]
+SIDES = [d for d in NEAR if max(d) > 0]
+ROOTS = 4
 GROUND = [(a, b, c) for a in (0, 1) for b in (0, 1) for c in range(NZ)]
 
 
@@ -52,10 +56,10 @@
 
 def kernel(
     adj_h, lin_h, stiff_h, anchor_h, tile_h, row_h, col_h, off_h,
-    def_o, dem_o,
+    parts_o, tiles_o, peak_o,
     adj_v, lin_v, stiff_v, anchor_v, tile_v, row_v, col_v, off_v,
-    AX, PA, PAE, WX, PW, PWE, EX, PS, PSE, TE, W16, DG, G, K1, K2, CE, P1, P2, P3,
-    RH, RL, CV,
+    AX, PA, PAE, WX, PW, PWE, EX, PS, PSE, TE, W16, DG, G, K1, CE, P1, P2, P3,
+    RH, RL, CV, CH, CL,
     load_sem, w_send, w_recv, a_send, a_recv, t_send, t_recv, s_send, s_recv,
     e_send, e_recv, p1_send, p1_recv, p2_send, p2_recv, p3_send, p3_recv,
 ):
@@ -64,8 +68,7 @@
     def at(dx, dy, dz):
         return (gx + dx, lax.rem(gy + dy + NY, NY), lax.rem(gz + dz + NZ, NZ))
 
-    first, last = gx == 0, gx == NX - 1
-    not_first, not_last = gx > 0, gx < NX - 1
+    not_first, not_last, is_root = gx > 0, gx < NX - 1, gx < ROOTS
     can_send = {0: None, 1: not_last, -1: not_first}
     can_receive = {0: None, 1: not_first, -1: not_last}
 
@@ -74,20 +77,26 @@
     def greet(device):
         pl.semaphore_signal(barrier, inc=1, device_id=device, device_id_type=MESH)
 
-    def greet_x(dx):
-        for dy in (-1, 0, 1):
-            for dz in (-1, 0, 1):
-                greet(at(dx, dy, dz))
-
+    def greet_near(steps):
+        for dx in (0, 1, -1):
+            these = [d for d in steps if d[0] == dx]
+
+            def go(these=these):
+                for d in these:
+                    greet(at(*d))
+
+            guarded(can_send[dx], go)
+
+    greet_near(DOWN)
+    greet_near(SIDES)
     for b, c in PLANE:
-        greet(at(0, b, c))
-    pl.when(not_first)(functools.partial(greet_x, -1))
-    pl.when(not_last)(functools.partial(greet_x, 1))
-
-    @pl.when(first)
+        if (0, (b + 1) % NY - 1, (c + 1) % NZ - 1) not in NEAR:
+            greet(at(0, b, c))
+
+    @pl.when(is_root)
     def _():
         for i in range(1, NX):
-            greet((i, gy, gz))
+            greet((lax.rem(gx + i, NX), gy, gz))
 
     loads = [
         pltpu.make_async_copy(h, v, load_sem.at[i])
@@ -132,7 +141,7 @@
 
     pl.semaphore_wait(
         barrier,
-        len(PLANE) + jnp.where(not_first, 10, 0) + jnp.where(not_last, 9, 0),
+        len(PLANE) + jnp.where(not_first, 9, 0) + jnp.where(not_last, 9, 0) + jnp.where(is_root, ROOTS - 1, ROOTS),
     )
 
     def w_copy(d):
@@ -170,8 +179,9 @@
             TE.at[0], TE.at[i], t_send.at[i], t_recv.at[i], device_id=at(a, b, 0), device_id_type=MESH
         )
 
-    w_copies = [(d[0], w_copy(d)) for d in sorted(NEAR, key=lambda d: -sum(x >= 0 for x in d))]
-    a_copies = [(d[0], a_copy(d)) for d in NEAR if max(d) <= 0]
+    w_up = [(d[0], w_copy(d)) for d in UP]
+    w_rest = [(d[0], w_copy(d)) for d in NEAR if d not in UP]
+    a_copies = [(d[0], a_copy(d)) for d in DOWN]
     t_copies = [(a, t_copy(a, b)) for a, b in ((0, 1), (1, 0), (1, 1))]
 
     def start_all(copies):
@@ -204,8 +214,9 @@
 
             guarded(can_send[step], go)
 
-    start_all(w_copies)
+    start_all(w_up)
     start_all(a_copies)
+    start_all(w_rest)
     start_all(t_copies)
 
     row16 = lax.broadcasted_iota(jnp.int32, (16, 256), 0)
@@ -226,24 +237,24 @@
     window16 = lax.broadcasted_iota(jnp.int32, (16, 128), 1)
     from_left = lax.rem(window16, 8) < 4
 
-    receive_all(w_copies)
-    for f in range(2):
-        for z in range(-2, 9):
-            slot, zz = (0, z + 8) if z < 0 else (1, z) if z < 8 else (2, z - 8)
-            mixed = jnp.where(from_left, PWE[0, slot], PWE[1, slot])
-            w = f * BZ + zz
-            WX[f, z + 2, :, 128:256] = pltpu.roll(mixed, (124 - 8 * w) % 128, 1)
-    for z in range(-2, 9):
-        W16[z + 2] = jnp.where(element_mask(z), WX[0, z + 2], 0.0) * (1.0 / 16.0)
-    highest = jnp.zeros((8, 128), F32)
-    for z in range(-1, 9):
-        total = W16[z + 1] + W16[z + 2]
-        total = total + pltpu.roll(total, 1, 0)
-        total = total + pltpu.roll(total, 1, 1)
-        spring = jnp.where(node_mask(z), WX[1, z + 2], 0.0)
-        DG[z + 1] = spring + 4.0 * total
-        if 0 <= z < 8:
-            highest = jnp.maximum(highest, (spring + 44.0 * total)[0:8, 0:128])
+    receive_all(w_up)
+    row8 = lax.broadcasted_iota(jnp.int32, (8, 128), 0)
+    here_x, here_y = gx * BX + row8 <= NX * BX - 2, gy * BY + lane <= NY * BY - 2
+    held, highest = None, jnp.zeros((8, 128), F32)
+    for z in range(-1, BZ):
+        slot, zz = (0, z + 8) if z < 0 else (1, z)
+        shift = (124 - 8 * zz) % 128
+        there = (gz * BZ + z >= 0) & (gz * BZ + z <= NZ * BZ - 2)
+        main = jnp.where(here_x & here_y & there, WX[0, z + 2, 0:8, 0:128], 0.0)
+        side = jnp.where(here_x & (gy > 0) & there, pltpu.roll(PWE[0, slot, 0:8], shift, 1), 0.0)
+        under = jnp.where(here_y[0:1] & not_first & there, WX[0, z + 2, 12:16, 0:128][3:4], 0.0)
+        corner = jnp.where(not_first & (gy > 0) & there, pltpu.roll(PWE[0, slot, 12:16], shift, 1)[3:4], 0.0)
+        main = main + jnp.where(row8 == 0, under, pltpu.roll(main, 1, 0))
+        side = side + jnp.where(row8 == 0, corner, pltpu.roll(side, 1, 0))
+        layer = main + jnp.where(lane == 0, pltpu.roll(side, 1, 1), pltpu.roll(main, 1, 1))
+        if held is not None:
+            highest = jnp.maximum(highest, anchor_v[z] + 2.75 * (held + layer))
+        held = layer
 
     P1[0:1] = jnp.max(highest, axis=0, keepdims=True)
     for b, c in PLANE:
@@ -303,6 +314,34 @@
     s_copies = [(d[0], s_copy(d)) for d in sorted(NEAR, key=lambda d: abs(d[1]))]
     start_all(s_copies)
 
+    pltpu.make_async_copy(P1.at[pl.ds(1, 31)], P1.at[pl.ds(1, 31)], p1_recv).wait()
+    P2[pl.ds(gx, 1)] = jnp.max(P1[...], axis=0, keepdims=True)
+    own = pl.ds(gx, 1)
+    ups = [
+        pltpu.make_async_remote_copy(
+            P2.at[own], P2.at[own], p2_send, p2_recv, device_id=(r, gy, gz), device_id_type=MESH
+        )
+        for r in range(ROOTS)
+    ]
+    for r in range(ROOTS):
+        pl.when(gx != r)(ups[r].start)
+
+    receive_all(w_rest)
+    for f in range(2):
+        for z in range(-2, 9):
+            slot, zz = (0, z + 8) if z < 0 else (1, z) if z < 8 else (2, z - 8)
+            mixed = jnp.where(from_left, PWE[0, slot], PWE[1, slot])
+            w = f * BZ + zz
+            WX[f, z + 2, :, 128:256] = pltpu.roll(mixed, (124 - 8 * w) % 128, 1)
+    for z in range(-2, 9):
+        W16[z + 2] = jnp.where(element_mask(z), WX[0, z + 2], 0.0) * (1.0 / 16.0)
+    for z in range(-1, 9):
+        total = W16[z + 1] + W16[z + 2]
+        total = total + pltpu.roll(total, 1, 0)
+        total = total + pltpu.roll(total, 1, 1)
+        spring = jnp.where(node_mask(z), WX[1, z + 2], 0.0)
+        DG[z + 1] = spring + 4.0 * total
+
     receive_all(t_copies)
     mine = (gx * NY + gy).astype(F32)
     rows = lax.broadcasted_iota(jnp.int32, (256, 128), 0).astype(F32)
@@ -325,14 +364,6 @@
             r, f = col_at[x : x + 1], fc[x : x + 1]
             CV[:, part] = jnp.where(columns == r, 1.0 - f, jnp.where(columns == r + 1.0, f, 0.0))
 
-    pltpu.make_async_copy(P1.at[pl.ds(1, 31)], P1.at[pl.ds(1, 31)], p1_recv).wait()
-    plane_highest = jnp.max(P1[...], axis=0, keepdims=True)
-    P2[0:1] = plane_highest
-    up = pltpu.make_async_remote_copy(
-        P2.at[pl.ds(0, 1)], P2.at[pl.ds(gx, 1)], p2_send, p2_recv, device_id=(0, gy, gz), device_id_type=MESH
-    )
-    pl.when(not_first)(up.start)
-
     receive_all(s_copies)
     for side_slot in range(1):
         mixed = [jnp.where(from_left, PSE[0, s], PSE[1, s]) for s in range(4)]
@@ -367,6 +398,9 @@
             G[0, z + 2] = behind_y(qx) + qx
             G[1, z + 2] = behind_y(qy) - qy
             G[2, z + 2] = behind_y(qz) + qz
+            if 0 <= z < BZ:
+                for c in range(3):
+                    parts_o[0, c, z] = G[c, z + 2, 0:8, 0:128]
         held = sense
 
     def element_forces(low, high, weight):
@@ -401,7 +435,10 @@
         plus, minus = element_forces([G[c, j] for c in range(3)], [G[c, j + 1] for c in range(3)], W16[j])
         if held is not None:
             for c in range(3):
-                K1[c, j - 1] = held[c] + minus[c] + DG[j - 1] * G[c, j]
+                value = held[c] + minus[c] + DG[j - 1] * G[c, j]
+                K1[c, j - 1] = value
+                if 0 <= j - 2 < BZ:
+                    parts_o[1, c, j - 2] = value[0:8, 0:128]
         held = plus
 
     sums = [jnp.zeros((8, 128), F32) for _ in range(3)]
@@ -412,11 +449,10 @@
             z = j - 1
             for c in range(3):
                 value = held[c] + minus[c] + DG[j] * K1[c, j]
-                K2[c, z] = value[0:8, 0:128]
+                parts_o[2, c, z] = value[0:8, 0:128]
             share = ((NZ * BZ - 1 - z) - gz * BZ).astype(F32) * (1.0 / (NZ * BZ - 1))
-            sums[0] = sums[0] + share * G[2, z + 2, 0:8, 0:128]
-            sums[1] = sums[1] + share * K1[2, z + 1, 0:8, 0:128]
-            sums[2] = sums[2] + share * K2[2, z]
+            for k in range(3):
+                sums[k] = sums[k] + share * parts_o[k, 2, z]
         held = plus
     for k in range(3):
         CE[0, k] = sums[k]
@@ -436,20 +472,68 @@
 
         guarded(can_send[a], go)
 
-    @pl.when(first)
+    pltpu.make_async_copy(CE.at[pl.ds(1, 7)], CE.at[pl.ds(1, 7)], e_recv.at[0]).wait()
+
+    @pl.when(not_first)
+    def _():
+        pltpu.make_async_copy(CE.at[pl.ds(8, 8)], CE.at[pl.ds(8, 8)], e_recv.at[1]).wait()
+
+    for q in range(4):
+        columns = [CE[4 * q, k] + CE[4 * q + 1, k] + CE[4 * q + 2, k] + CE[4 * q + 3, k] for k in range(3)]
+        if q >= 2:
+            columns = [jnp.where(not_first, column, 0.0) for column in columns]
+        for x in range(BX):
+            part = pl.ds((q * BX + x) * 128, 128)
+            for k in range(3):
+                value = CV[:, part] * columns[k][x : x + 1]
+                high = value.astype(BF16)
+                CH[k * 128 : k * 128 + 128, part] = high
+                CL[k * 128 : k * 128 + 128, part] = (value - high.astype(F32)).astype(BF16)
+    dims = (((1,), (1,)), ((), ()))
+
+    def times(a, b):
+        return lax.dot_general(a, b, dims, preferred_element_type=F32)
+
+    tiles = times(RH[...], CH[...]) + times(RH[...], CL[...]) + times(RL[...], CH[...])
+    for k in range(3):
+        tiles_o[k] = tiles[:, k * 128 : k * 128 + 128]
+
+    @pl.when(is_root)
     def _():
         pltpu.make_async_copy(P2.at[pl.ds(1, 15)], P2.at[pl.ds(1, 15)], p2_recv).wait()
         P3[...] = jnp.max(P2[...], axis=0, keepdims=True)
-        for i in range(1, NX):
+        for i in range(3):
             pltpu.make_async_remote_copy(
-                P3, P3, p3_send, p3_recv, device_id=(i, gy, gz), device_id_type=MESH
+                P3, P3, p3_send, p3_recv, device_id=(13 - 3 * gx + i, gy, gz), device_id_type=MESH
             ).start()
 
-    @pl.when(not_first)
+    @pl.when(jnp.logical_not(is_root))
     def _():
         pltpu.make_async_copy(P3, P3, p3_recv).wait()
 
-    top = jnp.max(P3[...], axis=1, keepdims=True)
+    peak_o[...] = jnp.broadcast_to(P3[...], (8, 128))
+
+    sent_all(w_up)
+    sent_all(w_rest)
+    sent_all(a_copies)
+    sent_all(t_copies)
+    sent_all(s_copies)
+    pltpu.make_async_copy(P1.at[pl.ds(1, 31)], P1.at[pl.ds(1, 31)], p1_send).wait()
+    for r in range(ROOTS):
+        pl.when(gx != r)(ups[r].wait_send)
+    pltpu.make_async_copy(CE.at[pl.ds(1, 7)], CE.at[pl.ds(1, 7)], e_send.at[0]).wait()
+
+    @pl.when(not_last)
+    def _():
+        pltpu.make_async_copy(CE.at[pl.ds(8, 8)], CE.at[pl.ds(8, 8)], e_send.at[1]).wait()
+
+    @pl.when(is_root)
+    def _():
+        pltpu.make_async_copy(P2.at[pl.ds(1, 3)], P2.at[pl.ds(1, 3)], p3_send).wait()
+
+
+def combine(parts, tiles, peak, def_o, dem_o):
+    top = jnp.max(peak[...], axis=1, keepdims=True)
     low = top / 30.0
     center = 0.5 * (top + low)
     half_width = 0.5 * (top - low)
@@ -467,63 +551,34 @@
     k0, k1, k2 = [jnp.broadcast_to(k, (8, 128)) for k in (k0, k1, k2)]
     for c in range(3):
         for z in range(BZ):
-            def_o[c, z] = k0 * G[c, z + 2, 0:8, 0:128] + k1 * K1[c, z + 1, 0:8, 0:128] + k2 * K2[c, z]
-
-    pltpu.make_async_copy(CE.at[pl.ds(1, 7)], CE.at[pl.ds(1, 7)], e_recv.at[0]).wait()
-
-    @pl.when(not_first)
-    def _():
-        pltpu.make_async_copy(CE.at[pl.ds(8, 8)], CE.at[pl.ds(8, 8)], e_recv.at[1]).wait()
-
-    result = jnp.zeros((256, 128), F32)
-    for q in range(4):
-        parts = [
-            CE[4 * q, k] + CE[4 * q + 1, k] + CE[4 * q + 2, k] + CE[4 * q + 3, k] for k in range(3)
-        ]
-        column = k0 * parts[0] + k1 * parts[1] + k2 * parts[2]
-        if q >= 2:
-            column = jnp.where(not_first, column, 0.0)
-        for x in range(BX):
-            part = pl.ds((q * BX + x) * 128, 128)
-            value = CV[:, part] * column[x : x + 1]
-            high = value.astype(BF16)
-            rest = (value - high.astype(F32)).astype(BF16)
-            both = jnp.concatenate([high, rest], axis=0)
-            dims = (((1,), (1,)), ((), ()))
-            pair = lax.dot_general(RH[:, part], both, dims, preferred_element_type=F32)
-            result = result + pair[:, 0:128] + pair[:, 128:256]
-            result = result + lax.dot_general(RL[:, part], high, dims, preferred_element_type=F32)
-    dem_o[...] = result
-
-    sent_all(w_copies)
-    sent_all(a_copies)
-    sent_all(t_copies)
-    sent_all(s_copies)
-    pltpu.make_async_copy(P1.at[pl.ds(1, 31)], P1.at[pl.ds(1, 31)], p1_send).wait()
-    pl.when(not_first)(up.wait_send)
-    pltpu.make_async_copy(CE.at[pl.ds(1, 7)], CE.at[pl.ds(1, 7)], e_send.at[0]).wait()
-
-    @pl.when(not_last)
-    def _():
-        pltpu.make_async_copy(CE.at[pl.ds(8, 8)], CE.at[pl.ds(8, 8)], e_send.at[1]).wait()
-
-    @pl.when(first)
-    def _():
-        pltpu.make_async_copy(P2.at[pl.ds(1, 15)], P2.at[pl.ds(1, 15)], p3_send).wait()
+            def_o[c, z] = k0 * parts[0, c, z] + k1 * parts[1, c, z] + k2 * parts[2, c, z]
+    for i in range(TILE_ROWS // 8):
+        part = pl.ds(8 * i, 8)
+        dem_o[part] = k0 * tiles[0, part] + k1 * tiles[1, part] + k2 * tiles[2, part]
 
 
 def per_device(adjoint, linearized, stiffness, anchor, target_tile, target_row, target_col, offsets):
     vmem = lambda *shape, dtype=F32: pltpu.VMEM(shape, dtype)
     dma = pltpu.SemaphoreType.DMA
     ground = (BX, BY)
-    return pl.pallas_call(
+    operands = [
+        pltpu.with_memory_space_constraint(x, pltpu.HBM)
+        for x in (
+            adjoint, linearized, stiffness, anchor,
+            target_tile.reshape(ground), target_row.reshape(ground), target_col.reshape(ground),
+            offsets.reshape((2,) + ground),
+        )
+    ]
+    whole = pl.BlockSpec(memory_space=pltpu.VMEM)
+    held = pl.pallas_call(
         kernel,
         out_shape=(
-            jax.ShapeDtypeStruct((3, BZ, BX, BY), F32),
-            jax.ShapeDtypeStruct((TILE_ROWS, TILE_COLUMNS), F32),
+            pltpu.VMEM((3, 3, BZ, BX, BY), F32),
+            pltpu.VMEM((3, TILE_ROWS, TILE_COLUMNS), F32),
+            pltpu.VMEM((8, 128), F32),
         ),
-        in_specs=[pl.BlockSpec(memory_space=pl.ANY)] * 8,
-        out_specs=[pl.BlockSpec(memory_space=pltpu.VMEM)] * 2,
+        in_specs=[pl.BlockSpec(memory_space=pltpu.HBM)] * 8,
+        out_specs=[whole] * 3,
         scratch_shapes=[
             vmem(6, BZ, BX, BY, dtype=BF16), vmem(18, BZ, BX, BY, dtype=BF16),
             vmem(BZ, BX, BY, dtype=BF16), vmem(BZ, BX, BY),
@@ -534,20 +589,26 @@
             vmem(3, SZ, 16, 256), vmem(2, 8, 128), vmem(2, 4, 16, 128),
             vmem(4, 5, 8, 128),
             vmem(WZ, 16, 256), vmem(10, 16, 256),
-            vmem(3, 12, 16, 256), vmem(3, 10, 16, 256), vmem(3, BZ, BX, BY),
+            vmem(3, 12, 16, 256), vmem(3, 10, 16, 256),
             vmem(16, 3, 8, 128), vmem(32, 128), vmem(16, 128), vmem(1, 128),
             vmem(256, 4096, dtype=BF16), vmem(256, 4096, dtype=BF16), vmem(128, 4096),
+            vmem(384, 4096, dtype=BF16), vmem(384, 4096, dtype=BF16),
             dma((8,)), dma((27,)), dma((27,)), dma((27,)), dma((27,)), dma((4,)), dma((4,)),
             dma((27,)), dma((27,)), dma((2,)), dma((2,)), dma, dma, dma, dma, dma, dma,
         ],
         compiler_params=pltpu.CompilerParams(
-            collective_id=0, has_side_effects=True, vmem_limit_bytes=48 * 1024 * 1024
+            collective_id=0, has_side_effects=True, vmem_limit_bytes=40 * 1024 * 1024
         ),
-    )(
-        adjoint, linearized, stiffness, anchor,
-        target_tile.reshape(ground), target_row.reshape(ground), target_col.reshape(ground),
-        offsets.reshape((2,) + ground),
-    )
+    )(*operands)
+    return pl.pallas_call(
+        combine,
+        out_shape=(
+            jax.ShapeDtypeStruct((3, BZ, BX, BY), F32),
+            jax.ShapeDtypeStruct((TILE_ROWS, TILE_COLUMNS), F32),
+        ),
+        in_specs=[whole] * 3,
+        out_specs=[whole] * 2,
+    )(*[pltpu.with_memory_space_constraint(x, pltpu.VMEM) for x in held])
 
 
 def solution(mesh):

time: 45.6 us -> 36.5 us (0.80)
  the two profiles are of different devices: /device:TPU:32 before, /device:TPU:128 now
where the time goes in v2:
time: 36.5 us; the launch traced here: 36.4 us
  Pallas kernels  35.7 us (98%)
  between operations  0.64 us (2%)
    pallas_call x1, Pallas kernels, per_device(): pl.pallas_call(kernel, out_shape=(pltpu.VMEM((3, 3, BZ, BX, BY), F32), pl...  34.9 us
    pallas_call x1, Pallas kernels, per_device(): pl.pallas_call(combine, out_shape=(jax.ShapeDtypeStruct((3, BZ, BX, BY),...  0.82 us

profile of v2, /device:TPU:128, one launch (start us, length us, event | category | flops | bytes accessed | tf_op | source)
XLA Modules:
  0.0 36.4 jit_solution(409647158616690044)
XLA Ops:
  0.6 34.9 %shard_map.95 = (f32[3,3,8,8,128]{4,3,2,1,0:T(8,128)S(1)}, f32[3,256,128]{2,1,0:T(8,128)S(1)}, f32[8,128]{1,0:T(8,128)S(1)}) custom-call(bf16[6,8,8,128]{3,2,1,0:T(8,128)(2,1)} %adj_h.1, bf16[18,8,8,128]{3,2,1,0:T(8,128)(2,1)} %lin_h.1, bf16[8,8,128]{2,1,0:T(8,128)(2,1)} %stiff_h.1, f32[8,8,128]{2,1,0:T(8,128)} %anchor_h.1, s32[8,128]{1,0:T(8,128)} %bitcast.5, ...), custom_call_target="tpu_custom_call" | custom-call | tf_op jit(solution)/shard_map/pallas_call | solution.py:573
  35.5 0.8 %shard_map.96 = (f32[3,8,8,128]{3,2,1,0:T(8,128)}, f32[256,128]{1,0:T(8,128)}) custom-call(f32[3,3,8,8,128]{4,3,2,1,0:T(8,128)S(1)} %get-tuple-element.5.parts, f32[3,256,128]{2,1,0:T(8,128)S(1)} %get-tuple-element.6.tiles, f32[8,128]{1,0:T(8,128)S(1)} %get-tuple-element.7.peak), custom_call_target="tpu_custom_call" | custom-call | tf_op jit(solution)/shard_map/pallas_call | solution.py:603

commit v3 on v2

--- a/solution.py
+++ b/solution.py
@@ -25,7 +25,10 @@
 DOWN = [d for d in NEAR if max(d) <= 0]
 UP = [d for d in NEAR if min(d) >= 0]
 SIDES = [d for d in NEAR if max(d) > 0]
+COLLECTORS = [(b, c) for b in range(1, NY, 2) for c in range(0, NZ, 2)]
+IMAGES_FIRST = 1
 ROOTS = 4
+SERVED = ((13, 14, 15), (), (9, 10, 11, 12), (4, 5, 6, 7, 8))
 GROUND = [(a, b, c) for a in (0, 1) for b in (0, 1) for c in range(NZ)]
 
 
@@ -40,10 +43,12 @@
         pl.when(condition)(act)
 
 
-def rows_between(dx):
+def rows_between(dx, below, above):
     if dx == 0:
         return pl.ds(0, 8), pl.ds(0, 8)
-    return (pl.ds(4, 4), pl.ds(12, 4)) if dx == 1 else (pl.ds(0, 4), pl.ds(8, 4))
+    if dx == 1:
+        return pl.ds(8 - below, below), pl.ds(16 - below, below)
+    return pl.ds(0, above), pl.ds(8, above)
 
 
 def layers_between(dz, below, above):
@@ -54,12 +59,28 @@
     return pl.ds(0, above), pl.ds(below + BZ, above)
 
 
+def sweep_factors(maxima):
+    top = jnp.broadcast_to(jnp.max(maxima, axis=1, keepdims=True), (8, 128))
+    low = top / 30.0
+    center = 0.5 * (top + low)
+    half_width = 0.5 * (top - low)
+    ratio = center / half_width
+    rho0 = 1.0 / ratio
+    rho1 = 1.0 / (2.0 * ratio - rho0)
+    rho2 = 1.0 / (2.0 * ratio - rho1)
+    inverse = 1.0 / center
+    a1, b1 = rho1 * rho0, 2.0 * rho1 / half_width
+    a2, b2 = rho2 * rho1, 2.0 * rho2 / half_width
+    p, q = a1 * inverse + b1, -b1 * inverse
+    return inverse + p + a2 * p + b2, q + a2 * q - b2 * (inverse + p), -b2 * q
+
+
 def kernel(
     adj_h, lin_h, stiff_h, anchor_h, tile_h, row_h, col_h, off_h,
-    parts_o, tiles_o, peak_o,
+    parts_o, tiles_o, factors_o,
     adj_v, lin_v, stiff_v, anchor_v, tile_v, row_v, col_v, off_v,
-    AX, PA, PAE, WX, PW, PWE, EX, PS, PSE, TE, W16, DG, G, K1, CE, P1, P2, P3,
-    RH, RL, CV, CH, CL,
+    AX, PA, PAE, WX, PW, PWE, EX, PS, PSE, TE, TG, W16, DG, G, K1, CE, CS, P1, P2, P3,
+    RH, RL, CH, CL,
     load_sem, w_send, w_recv, a_send, a_recv, t_send, t_recv, s_send, s_recv,
     e_send, e_recv, p1_send, p1_recv, p2_send, p2_recv, p3_send, p3_recv,
 ):
@@ -69,34 +90,9 @@
         return (gx + dx, lax.rem(gy + dy + NY, NY), lax.rem(gz + dz + NZ, NZ))
 
     not_first, not_last, is_root = gx > 0, gx < NX - 1, gx < ROOTS
+    is_collector = (lax.rem(gy, 2) == 1) & (lax.rem(gz, 2) == 0)
     can_send = {0: None, 1: not_last, -1: not_first}
     can_receive = {0: None, 1: not_first, -1: not_last}
-
-    barrier = pltpu.get_barrier_semaphore()
-
-    def greet(device):
-        pl.semaphore_signal(barrier, inc=1, device_id=device, device_id_type=MESH)
-
-    def greet_near(steps):
-        for dx in (0, 1, -1):
-            these = [d for d in steps if d[0] == dx]
-
-            def go(these=these):
-                for d in these:
-                    greet(at(*d))
-
-            guarded(can_send[dx], go)
-
-    greet_near(DOWN)
-    greet_near(SIDES)
-    for b, c in PLANE:
-        if (0, (b + 1) % NY - 1, (c + 1) % NZ - 1) not in NEAR:
-            greet(at(0, b, c))
-
-    @pl.when(is_root)
-    def _():
-        for i in range(1, NX):
-            greet((lax.rem(gx + i, NX), gy, gz))
 
     loads = [
         pltpu.make_async_copy(h, v, load_sem.at[i])
@@ -105,7 +101,39 @@
              (row_h, row_v), (col_h, col_v), (off_h, off_v), (lin_h, lin_v))
         )
     ]
-    for copy in loads:
+    for copy in loads[:2]:
+        copy.start()
+
+    barrier = pltpu.get_barrier_semaphore()
+
+    def greet(device):
+        pl.semaphore_signal(barrier, inc=1, device_id=device, device_id_type=MESH)
+
+    def greet_near(steps):
+        for dx in (0, 1, -1):
+            these = [d for d in steps if d[0] == dx]
+
+            def go(these=these):
+                for d in these:
+                    greet(at(*d))
+
+            guarded(can_send[dx], go)
+
+    greet_near(DOWN)
+    greet_near(SIDES)
+
+    @pl.when(is_collector)
+    def _():
+        for b, c in PLANE:
+            if (0, (b + 1) % NY - 1, (c + 1) % NZ - 1) not in NEAR:
+                greet(at(0, b, c))
+
+    @pl.when(is_root)
+    def _():
+        for i in range(1, NX):
+            greet((lax.rem(gx + i, NX), gy + 1 - lax.rem(gy, 2), gz - lax.rem(gz, 2)))
+
+    for copy in loads[2:]:
         copy.start()
 
     lane = lax.broadcasted_iota(jnp.int32, (8, 128), 1)
@@ -121,44 +149,26 @@
             packed = jnp.where(lane // 8 == w, pltpu.roll(values[z], (8 * w + 4) % 128, 1), packed)
     PW[...] = packed
 
-    loads[2].wait()
-    packed = jnp.zeros((8, 128), F32)
-    for v in range(VARIABLES):
-        values = adj_v[v].astype(F32)
-        AX[v, 0:8, 0:8, 0:128] = values
-        for z in range(BZ):
-            w = v * BZ + z
-            packed = jnp.where(lane == w, pltpu.roll(values[z], w, 1), packed)
-    PA[...] = packed
-
-    for i in range(3, 7):
-        loads[i].wait()
-    TE[0, 0] = tile_v[...].astype(F32)
-    TE[0, 1] = row_v[...].astype(F32)
-    TE[0, 2] = col_v[...].astype(F32)
-    TE[0, 3] = off_v[0]
-    TE[0, 4] = off_v[1]
-
     pl.semaphore_wait(
         barrier,
-        len(PLANE) + jnp.where(not_first, 9, 0) + jnp.where(not_last, 9, 0) + jnp.where(is_root, ROOTS - 1, ROOTS),
+        8 + jnp.where(not_first, 9, 0) + jnp.where(not_last, 9, 0)
+        + len(COLLECTORS) - (2 - lax.rem(gy, 2)) * (1 + lax.rem(gz, 2))
+        + jnp.where(is_collector, jnp.where(is_root, 4 * ROOTS - 4, 4 * ROOTS), 0),
     )
 
-    def w_copy(d):
+    def w_copy(d, fields=slice(0, 2), below=2):
         dx, dy, dz = d
-        rs, rd = rows_between(dx)
+        rs, rd = rows_between(dx, below, 1)
         if dy == 0:
-            zs, zd = layers_between(dz, 2, 1)
-            src, dst = WX.at[:, pl.ds(2 + zs.start, zs.size), rs, 0:128], WX.at[:, zd, rs_at(rd), 0:128]
+            zs, zd = layers_between(dz, below, 1)
+            zs, zd = pl.ds(2 + zs.start, zs.size), pl.ds(2 - below + zd.start, zd.size)
+            src, dst = WX.at[fields, zs, rs, 0:128], WX.at[fields, zd, rd, 0:128]
         else:
             src, dst = PW.at[rs], PWE.at[0 if dy == 1 else 1, 1 - dz, rd]
-        i = near_index(d)
+        i = near_index(d) if fields != slice(1, 2) else 27 + near_index(d)
         return pltpu.make_async_remote_copy(
             src, dst, w_send.at[i], w_recv.at[i], device_id=at(*d), device_id_type=MESH
         )
-
-    def rs_at(rd):
-        return rd
 
     def a_copy(d):
         dx, dy, dz = d
@@ -179,8 +189,9 @@
             TE.at[0], TE.at[i], t_send.at[i], t_recv.at[i], device_id=at(a, b, 0), device_id_type=MESH
         )
 
-    w_up = [(d[0], w_copy(d)) for d in UP]
+    w_up = [(d[0], w_copy(d, slice(0, 1)) if d[1] == 0 else w_copy(d)) for d in UP]
     w_rest = [(d[0], w_copy(d)) for d in NEAR if d not in UP]
+    w_rest += [(d[0], w_copy(d, slice(1, 2), 1)) for d in UP if d[1] == 0]
     a_copies = [(d[0], a_copy(d)) for d in DOWN]
     t_copies = [(a, t_copy(a, b)) for a, b in ((0, 1), (1, 0), (1, 1))]
 
@@ -215,6 +226,25 @@
             guarded(can_send[step], go)
 
     start_all(w_up)
+
+    loads[2].wait()
+    packed = jnp.zeros((8, 128), F32)
+    for v in range(VARIABLES):
+        values = adj_v[v].astype(F32)
+        AX[v, 0:8, 0:8, 0:128] = values
+        for z in range(BZ):
+            w = v * BZ + z
+            packed = jnp.where(lane == w, pltpu.roll(values[z], w, 1), packed)
+    PA[...] = packed
+
+    for i in range(3, 7):
+        loads[i].wait()
+    TE[0, 0] = tile_v[...].astype(F32)
+    TE[0, 1] = row_v[...].astype(F32)
+    TE[0, 2] = col_v[...].astype(F32)
+    TE[0, 3] = off_v[0]
+    TE[0, 4] = off_v[1]
+
     start_all(a_copies)
     start_all(w_rest)
     start_all(t_copies)
@@ -256,12 +286,13 @@
             highest = jnp.maximum(highest, anchor_v[z] + 2.75 * (held + layer))
         held = layer
 
-    P1[0:1] = jnp.max(highest, axis=0, keepdims=True)
-    for b, c in PLANE:
-        i = b * NZ + c
-        pltpu.make_async_remote_copy(
-            P1.at[pl.ds(0, 1)], P1.at[pl.ds(i, 1)], p1_send, p1_recv, device_id=at(0, b, c), device_id_type=MESH
-        ).start()
+    mine_in_plane = pl.ds(gy * NZ + gz, 1)
+    P1[mine_in_plane] = jnp.max(highest, axis=0, keepdims=True)
+    for b, c in COLLECTORS:
+        tell = pltpu.make_async_remote_copy(
+            P1.at[mine_in_plane], P1.at[mine_in_plane], p1_send, p1_recv, device_id=(gx, b, c), device_id_type=MESH
+        )
+        pl.when((gy != b) | (gz != c))(tell.start)
 
     receive_all(a_copies)
     loads[7].wait()
@@ -295,7 +326,7 @@
 
     def s_copy(d):
         dx, dy, dz = d
-        rs, rd = rows_between(dx)
+        rs, rd = rows_between(dx, 3, 2)
         if dy == 0:
             zs, zd = layers_between(dz, 3, 2)
             src = EX.at[:, pl.ds(3 + zs.start, zs.size), rs, 0:128]
@@ -313,18 +344,6 @@
 
     s_copies = [(d[0], s_copy(d)) for d in sorted(NEAR, key=lambda d: abs(d[1]))]
     start_all(s_copies)
-
-    pltpu.make_async_copy(P1.at[pl.ds(1, 31)], P1.at[pl.ds(1, 31)], p1_recv).wait()
-    P2[pl.ds(gx, 1)] = jnp.max(P1[...], axis=0, keepdims=True)
-    own = pl.ds(gx, 1)
-    ups = [
-        pltpu.make_async_remote_copy(
-            P2.at[own], P2.at[own], p2_send, p2_recv, device_id=(r, gy, gz), device_id_type=MESH
-        )
-        for r in range(ROOTS)
-    ]
-    for r in range(ROOTS):
-        pl.when(gx != r)(ups[r].start)
 
     receive_all(w_rest)
     for f in range(2):
@@ -344,25 +363,46 @@
 
     receive_all(t_copies)
     mine = (gx * NY + gy).astype(F32)
-    rows = lax.broadcasted_iota(jnp.int32, (256, 128), 0).astype(F32)
-    columns = lax.broadcasted_iota(jnp.int32, (128, 128), 0).astype(F32)
+    rows = lax.broadcasted_iota(jnp.int32, (256, 128), 0).astype(F32).astype(BF16)
+    nothing = jnp.zeros((256, 128), BF16)
+
+    def halves(value):
+        high = value.astype(BF16)
+        return high, (value - high.astype(F32)).astype(BF16)
+
     for q in range(4):
         here = TE[q, 0] == mine
         if q >= 2:
             here = here & not_first
         row_at = jnp.where(here, TE[q, 1], -9.0)
-        col_at = jnp.where(here, TE[q, 2], -9.0)
+        TG[q, 0] = jnp.where(here, TE[q, 2], -9.0)
         fr = jnp.where(here, TE[q, 3], 0.0)
-        fc = jnp.where(here, TE[q, 4], 0.0)
+        TG[q, 1] = jnp.where(here, TE[q, 4], 0.0)
+        at0, at1 = row_at.astype(BF16), (row_at + 1.0).astype(BF16)
+        (h0, l0), (h1, l1) = halves(1.0 - fr), halves(fr)
         for x in range(BX):
             part = pl.ds((q * BX + x) * 128, 128)
-            r, f = row_at[x : x + 1], fr[x : x + 1]
-            value = jnp.where(rows == r, 1.0 - f, jnp.where(rows == r + 1.0, f, 0.0))
-            high = value.astype(BF16)
-            RH[:, part] = high
-            RL[:, part] = (value - high.astype(F32)).astype(BF16)
-            r, f = col_at[x : x + 1], fc[x : x + 1]
-            CV[:, part] = jnp.where(columns == r, 1.0 - f, jnp.where(columns == r + 1.0, f, 0.0))
+            one, two = rows == at0[x : x + 1], rows == at1[x : x + 1]
+            RH[:, part] = jnp.where(one, h0[x : x + 1], jnp.where(two, h1[x : x + 1], nothing))
+            RL[:, part] = jnp.where(one, l0[x : x + 1], jnp.where(two, l1[x : x + 1], nothing))
+
+    own = pl.ds(gx, 1)
+    ups = [
+        pltpu.make_async_remote_copy(
+            P2.at[own], P2.at[own], p2_send, p2_recv, device_id=(r, gy - b, gz + c), device_id_type=MESH
+        )
+        for b in (0, 1) for c in (0, 1) for r in range(ROOTS)
+    ]
+
+    @pl.when(is_collector)
+    def _():
+        pltpu.make_async_copy(P1.at[pl.ds(1, 31)], P1.at[pl.ds(1, 31)], p1_recv).wait()
+        P2[own] = jnp.max(P1[...], axis=0, keepdims=True)
+        for i in sorted(range(4 * ROOTS), key=lambda i: i % ROOTS):
+            if i < ROOTS:
+                pl.when(gx != i)(ups[i].start)
+            else:
+                ups[i].start()
 
     receive_all(s_copies)
     for side_slot in range(1):
@@ -472,6 +512,26 @@
 
         guarded(can_send[a], go)
 
+    def wait_rows(count, semaphore):
+        pltpu.make_async_copy(P1.at[pl.ds(0, count)], P1.at[pl.ds(0, count)], semaphore).wait()
+
+    def root_step():
+        pl.when(is_collector)(lambda: wait_rows(NX - 1, p2_recv))
+        pl.when(jnp.logical_not(is_collector))(lambda: wait_rows(NX, p2_recv))
+        P3[...] = jnp.max(P2[...], axis=0, keepdims=True)
+        for r, served in enumerate(SERVED):
+
+            @pl.when(gx == r)
+            def _(served=served):
+                for i in served:
+                    pltpu.make_async_remote_copy(
+                        P3, P3, p3_send, p3_recv, device_id=(i, gy, gz), device_id_type=MESH
+                    ).start()
+
+    images_first = gx < IMAGES_FIRST
+
+    pl.when(is_root & jnp.logical_not(images_first))(root_step)
+
     pltpu.make_async_copy(CE.at[pl.ds(1, 7)], CE.at[pl.ds(1, 7)], e_recv.at[0]).wait()
 
     @pl.when(not_first)
@@ -479,79 +539,88 @@
         pltpu.make_async_copy(CE.at[pl.ds(8, 8)], CE.at[pl.ds(8, 8)], e_recv.at[1]).wait()
 
     for q in range(4):
-        columns = [CE[4 * q, k] + CE[4 * q + 1, k] + CE[4 * q + 2, k] + CE[4 * q + 3, k] for k in range(3)]
-        if q >= 2:
-            columns = [jnp.where(not_first, column, 0.0) for column in columns]
-        for x in range(BX):
-            part = pl.ds((q * BX + x) * 128, 128)
-            for k in range(3):
-                value = CV[:, part] * columns[k][x : x + 1]
-                high = value.astype(BF16)
-                CH[k * 128 : k * 128 + 128, part] = high
-                CL[k * 128 : k * 128 + 128, part] = (value - high.astype(F32)).astype(BF16)
-    dims = (((1,), (1,)), ((), ()))
+        for k in range(3):
+            column = CE[4 * q, k] + CE[4 * q + 1, k] + CE[4 * q + 2, k] + CE[4 * q + 3, k]
+            CS[q, k] = column if q < 2 else jnp.where(not_first, column, 0.0)
 
     def times(a, b):
-        return lax.dot_general(a, b, dims, preferred_element_type=F32)
-
-    tiles = times(RH[...], CH[...]) + times(RH[...], CL[...]) + times(RL[...], CH[...])
-    for k in range(3):
-        tiles_o[k] = tiles[:, k * 128 : k * 128 + 128]
-
-    @pl.when(is_root)
-    def _():
-        pltpu.make_async_copy(P2.at[pl.ds(1, 15)], P2.at[pl.ds(1, 15)], p2_recv).wait()
-        P3[...] = jnp.max(P2[...], axis=0, keepdims=True)
-        for i in range(3):
-            pltpu.make_async_remote_copy(
-                P3, P3, p3_send, p3_recv, device_id=(13 - 3 * gx + i, gy, gz), device_id_type=MESH
-            ).start()
-
-    @pl.when(jnp.logical_not(is_root))
-    def _():
-        pltpu.make_async_copy(P3, P3, p3_recv).wait()
-
-    peak_o[...] = jnp.broadcast_to(P3[...], (8, 128))
+        return lax.dot_general(a, b, (((1,), (1,)), ((), ())), preferred_element_type=F32)
+
+    def image(count, column_of):
+        for q in range(4):
+            fc = TG[q, 1]
+            at0, at1 = TG[q, 0].astype(BF16), (TG[q, 0] + 1.0).astype(BF16)
+            values = []
+            for k in range(count):
+                column = column_of(q, k)
+                values.append(halves(column * (1.0 - fc)) + halves(column * fc))
+            for x in range(BX):
+                part = pl.ds((q * BX + x) * 128, 128)
+                one, two = rows[0:128] == at0[x : x + 1], rows[0:128] == at1[x : x + 1]
+                for k in range(count):
+                    h0, l0, h1, l1 = [value[x : x + 1] for value in values[k]]
+                    own = pl.ds(k * 128, 128)
+                    CH[own, part] = jnp.where(one, h0, jnp.where(two, h1, nothing[0:128]))
+                    CL[own, part] = jnp.where(one, l0, jnp.where(two, l1, nothing[0:128]))
+        span = pl.ds(0, count * 128)
+        return times(RH[...], CH[span]) + times(RH[...], CL[span]) + times(RL[...], CH[span])
+
+    @pl.when(images_first)
+    def _():
+        tiles = image(3, lambda q, k: CS[q, k])
+        for k in range(3):
+            tiles_o[k] = tiles[:, k * 128 : k * 128 + 128]
 
     sent_all(w_up)
     sent_all(w_rest)
     sent_all(a_copies)
     sent_all(t_copies)
     sent_all(s_copies)
-    pltpu.make_async_copy(P1.at[pl.ds(1, 31)], P1.at[pl.ds(1, 31)], p1_send).wait()
-    for r in range(ROOTS):
-        pl.when(gx != r)(ups[r].wait_send)
+    @pl.when(is_collector)
+    def _():
+        wait_rows(len(COLLECTORS) - 1, p1_send)
+        pl.when(is_root)(lambda: wait_rows(4 * ROOTS - 1, p2_send))
+        pl.when(jnp.logical_not(is_root))(lambda: wait_rows(4 * ROOTS, p2_send))
+
+    @pl.when(jnp.logical_not(is_collector))
+    def _():
+        wait_rows(len(COLLECTORS), p1_send)
+
     pltpu.make_async_copy(CE.at[pl.ds(1, 7)], CE.at[pl.ds(1, 7)], e_send.at[0]).wait()
 
     @pl.when(not_last)
     def _():
         pltpu.make_async_copy(CE.at[pl.ds(8, 8)], CE.at[pl.ds(8, 8)], e_send.at[1]).wait()
 
+    pl.when(images_first)(root_step)
+
+    @pl.when(jnp.logical_not(is_root))
+    def _():
+        pltpu.make_async_copy(P3, P3, p3_recv).wait()
+
+    k0, k1, k2 = sweep_factors(jnp.broadcast_to(P3[...], (8, 128)))
+    for i, k in enumerate((k0, k1, k2)):
+        factors_o[i] = k
+        factors_o[3 + i] = jnp.where(images_first, k, 1.0 if i == 0 else 0.0)
+
+    @pl.when(jnp.logical_not(images_first))
+    def _():
+        tiles_o[0] = image(1, lambda q, k: k0 * CS[q, 0] + k1 * CS[q, 1] + k2 * CS[q, 2])
+        tiles_o[1:3] = jnp.zeros((2, TILE_ROWS, TILE_COLUMNS), F32)
+
     @pl.when(is_root)
     def _():
-        pltpu.make_async_copy(P2.at[pl.ds(1, 3)], P2.at[pl.ds(1, 3)], p3_send).wait()
-
-
-def combine(parts, tiles, peak, def_o, dem_o):
-    top = jnp.max(peak[...], axis=1, keepdims=True)
-    low = top / 30.0
-    center = 0.5 * (top + low)
-    half_width = 0.5 * (top - low)
-    ratio = center / half_width
-    rho0 = 1.0 / ratio
-    rho1 = 1.0 / (2.0 * ratio - rho0)
-    rho2 = 1.0 / (2.0 * ratio - rho1)
-    inverse = 1.0 / center
-    a1, b1 = rho1 * rho0, 2.0 * rho1 / half_width
-    a2, b2 = rho2 * rho1, 2.0 * rho2 / half_width
-    p, q = a1 * inverse + b1, -b1 * inverse
-    k0 = inverse + p + a2 * p + b2
-    k1 = q + a2 * q - b2 * (inverse + p)
-    k2 = -b2 * q
-    k0, k1, k2 = [jnp.broadcast_to(k, (8, 128)) for k in (k0, k1, k2)]
+        for r, served in enumerate(SERVED):
+            if served:
+                pl.when(gx == r)(functools.partial(wait_rows, len(served), p3_send))
+
+
+def combine(parts, tiles, factors, def_o, dem_o):
+    k0, k1, k2 = factors[0], factors[1], factors[2]
     for c in range(3):
         for z in range(BZ):
             def_o[c, z] = k0 * parts[0, c, z] + k1 * parts[1, c, z] + k2 * parts[2, c, z]
+    k0, k1, k2 = factors[3], factors[4], factors[5]
     for i in range(TILE_ROWS // 8):
         part = pl.ds(8 * i, 8)
         dem_o[part] = k0 * tiles[0, part] + k1 * tiles[1, part] + k2 * tiles[2, part]
@@ -575,7 +644,7 @@
         out_shape=(
             pltpu.VMEM((3, 3, BZ, BX, BY), F32),
             pltpu.VMEM((3, TILE_ROWS, TILE_COLUMNS), F32),
-            pltpu.VMEM((8, 128), F32),
+            pltpu.VMEM((6, 8, 128), F32),
         ),
         in_specs=[pl.BlockSpec(memory_space=pltpu.HBM)] * 8,
         out_specs=[whole] * 3,
@@ -587,13 +656,13 @@
             vmem(VARIABLES, AZ, 16, 256), vmem(8, 128), vmem(2, 16, 128),
             vmem(2, WZ, 16, 256), vmem(8, 128), vmem(2, 3, 16, 128),
             vmem(3, SZ, 16, 256), vmem(2, 8, 128), vmem(2, 4, 16, 128),
-            vmem(4, 5, 8, 128),
+            vmem(4, 5, 8, 128), vmem(4, 2, 8, 128),
             vmem(WZ, 16, 256), vmem(10, 16, 256),
             vmem(3, 12, 16, 256), vmem(3, 10, 16, 256),
-            vmem(16, 3, 8, 128), vmem(32, 128), vmem(16, 128), vmem(1, 128),
-            vmem(256, 4096, dtype=BF16), vmem(256, 4096, dtype=BF16), vmem(128, 4096),
+            vmem(16, 3, 8, 128), vmem(4, 3, 8, 128), vmem(32, 128), vmem(16, 128), vmem(1, 128),
+            vmem(256, 4096, dtype=BF16), vmem(256, 4096, dtype=BF16),
             vmem(384, 4096, dtype=BF16), vmem(384, 4096, dtype=BF16),
-            dma((8,)), dma((27,)), dma((27,)), dma((27,)), dma((27,)), dma((4,)), dma((4,)),
+            dma((8,)), dma((54,)), dma((54,)), dma((27,)), dma((27,)), dma((4,)), dma((4,)),
             dma((27,)), dma((27,)), dma((2,)), dma((2,)), dma, dma, dma, dma, dma, dma,
         ],
         compiler_params=pltpu.CompilerParams(

time: 36.5 us -> 34.1 us (0.934)
  the two profiles are of different devices: /device:TPU:128 before, /device:TPU:1 now
where the time goes in v3:
time: 34.1 us; the launch traced here: 33.9 us
  Pallas kernels  33.3 us (98%)
  between operations  0.64 us (2%)
    pallas_call x1, Pallas kernels, per_device(): pl.pallas_call(kernel, out_shape=(pltpu.VMEM((3, 3, BZ, BX, BY), F32), pl...  32.6 us
    pallas_call x1, Pallas kernels, per_device(): pl.pallas_call(combine, out_shape=(jax.ShapeDtypeStruct((3, BZ, BX, BY),...  0.72 us

profile of v3, /device:TPU:1, one launch (start us, length us, event | category | flops | bytes accessed | tf_op | source)
XLA Modules:
  0.0 33.9 jit_solution(1282804744172309341)
XLA Ops:
  0.6 32.6 %shard_map.95 = (f32[3,3,8,8,128]{4,3,2,1,0:T(8,128)S(1)}, f32[3,256,128]{2,1,0:T(8,128)S(1)}, f32[6,8,128]{2,1,0:T(8,128)S(1)}) custom-call(bf16[6,8,8,128]{3,2,1,0:T(8,128)(2,1)} %adj_h.1, bf16[18,8,8,128]{3,2,1,0:T(8,128)(2,1)} %lin_h.1, bf16[8,8,128]{2,1,0:T(8,128)(2,1)} %stiff_h.1, f32[8,8,128]{2,1,0:T(8,128)} %anchor_h.1, s32[8,128]{1,0:T(8,128)} %bitcast.5, ...), custom_call_target="tpu_custom_call" | custom-call | tf_op jit(solution)/shard_map/pallas_call | solution.py:642
  33.2 0.7 %shard_map.96 = (f32[3,8,8,128]{3,2,1,0:T(8,128)}, f32[256,128]{1,0:T(8,128)}) custom-call(f32[3,3,8,8,128]{4,3,2,1,0:T(8,128)S(1)} %get-tuple-element.5.parts, f32[3,256,128]{2,1,0:T(8,128)S(1)} %get-tuple-element.6.tiles, f32[6,8,128]{2,1,0:T(8,128)S(1)} %get-tuple-element.7.factors), custom_call_target="tpu_custom_call" | custom-call | tf_op jit(solution)/shard_map/pallas_call | solution.py:672

commit v4 on v3

--- a/solution.py
+++ b/solution.py
@@ -189,14 +189,14 @@
             TE.at[0], TE.at[i], t_send.at[i], t_recv.at[i], device_id=at(a, b, 0), device_id_type=MESH
         )
 
-    w_up = [(d[0], w_copy(d, slice(0, 1)) if d[1] == 0 else w_copy(d)) for d in UP]
+    w_up = [(d[0], w_copy(d, slice(0, 1)) if d[1] == 0 else w_copy(d)) for d in sorted(UP, key=lambda d: -sum(d))]
     w_rest = [(d[0], w_copy(d)) for d in NEAR if d not in UP]
     w_rest += [(d[0], w_copy(d, slice(1, 2), 1)) for d in UP if d[1] == 0]
-    a_copies = [(d[0], a_copy(d)) for d in DOWN]
+    a_copies = [(d[0], a_copy(d)) for d in sorted(DOWN, key=sum)]
     t_copies = [(a, t_copy(a, b)) for a, b in ((0, 1), (1, 0), (1, 1))]
 
     def start_all(copies):
-        for step in (0, 1, -1):
+        for step in (1, -1, 0):
             these = [c for dx, c in copies if dx == step]
 
             def go(these=these):
@@ -342,7 +342,7 @@
             src, dst, s_send.at[i], s_recv.at[i], device_id=at(*d), device_id_type=MESH
         )
 
-    s_copies = [(d[0], s_copy(d)) for d in sorted(NEAR, key=lambda d: abs(d[1]))]
+    s_copies = [(d[0], s_copy(d)) for d in sorted(NEAR, key=lambda d: -sum(abs(x) for x in d))]
     start_all(s_copies)
 
     receive_all(w_rest)
@@ -361,6 +361,24 @@
         spring = jnp.where(node_mask(z), WX[1, z + 2], 0.0)
         DG[z + 1] = spring + 4.0 * total
 
+    own = pl.ds(gx, 1)
+    ups = [
+        pltpu.make_async_remote_copy(
+            P2.at[own], P2.at[own], p2_send, p2_recv, device_id=(r, gy - b, gz + c), device_id_type=MESH
+        )
+        for b in (0, 1) for c in (0, 1) for r in range(ROOTS)
+    ]
+
+    @pl.when(is_collector)
+    def _():
+        pltpu.make_async_copy(P1.at[pl.ds(1, 31)], P1.at[pl.ds(1, 31)], p1_recv).wait()
+        P2[own] = jnp.max(P1[...], axis=0, keepdims=True)
+        for i in sorted(range(4 * ROOTS), key=lambda i: i % ROOTS):
+            if i < ROOTS:
+                pl.when(gx != i)(ups[i].start)
+            else:
+                ups[i].start()
+
     receive_all(t_copies)
     mine = (gx * NY + gy).astype(F32)
     rows = lax.broadcasted_iota(jnp.int32, (256, 128), 0).astype(F32).astype(BF16)
@@ -385,24 +403,6 @@
             one, two = rows == at0[x : x + 1], rows == at1[x : x + 1]
             RH[:, part] = jnp.where(one, h0[x : x + 1], jnp.where(two, h1[x : x + 1], nothing))
             RL[:, part] = jnp.where(one, l0[x : x + 1], jnp.where(two, l1[x : x + 1], nothing))
-
-    own = pl.ds(gx, 1)
-    ups = [
-        pltpu.make_async_remote_copy(
-            P2.at[own], P2.at[own], p2_send, p2_recv, device_id=(r, gy - b, gz + c), device_id_type=MESH
-        )
-        for b in (0, 1) for c in (0, 1) for r in range(ROOTS)
-    ]
-
-    @pl.when(is_collector)
-    def _():
-        pltpu.make_async_copy(P1.at[pl.ds(1, 31)], P1.at[pl.ds(1, 31)], p1_recv).wait()
-        P2[own] = jnp.max(P1[...], axis=0, keepdims=True)
-        for i in sorted(range(4 * ROOTS), key=lambda i: i % ROOTS):
-            if i < ROOTS:
-                pl.when(gx != i)(ups[i].start)
-            else:
-                ups[i].start()
 
     receive_all(s_copies)
     for side_slot in range(1):
@@ -503,8 +503,9 @@
             CE.at[0], CE.at[i], e_send.at[a], e_recv.at[a], device_id=at(a, b, c), device_id_type=MESH
         )
 
-    for a in (0, 1):
-        these = [e_copy(*d) for d in GROUND if d[0] == a and d != (0, 0, 0)]
+    for a in (1, 0):
+        far = sorted(GROUND, key=lambda d: -(d[1] + min(d[2], NZ - d[2])))
+        these = [e_copy(*d) for d in far if d[0] == a and d != (0, 0, 0)]
 
         def go(these=these):
             for copy in these:

time: 34.1 us -> 34 us (level)
  no operation moved by 1% of the time
where the time goes in v4:
time: 34 us; the launch traced here: 33.9 us
  Pallas kernels  33.2 us (98%)
  between operations  0.64 us (2%)
    pallas_call x1, Pallas kernels, per_device(): pl.pallas_call(kernel, out_shape=(pltpu.VMEM((3, 3, BZ, BX, BY), F32), pl...  32.5 us
    pallas_call x1, Pallas kernels, per_device(): pl.pallas_call(combine, out_shape=(jax.ShapeDtypeStruct((3, BZ, BX, BY),...  0.72 us

profile of v4, /device:TPU:1, one launch (start us, length us, event | category | flops | bytes accessed | tf_op | source)
XLA Modules:
  0.0 33.9 jit_solution(1454444707425655640)
XLA Ops:
  0.6 32.5 %shard_map.95 = (f32[3,3,8,8,128]{4,3,2,1,0:T(8,128)S(1)}, f32[3,256,128]{2,1,0:T(8,128)S(1)}, f32[6,8,128]{2,1,0:T(8,128)S(1)}) custom-call(bf16[6,8,8,128]{3,2,1,0:T(8,128)(2,1)} %adj_h.1, bf16[18,8,8,128]{3,2,1,0:T(8,128)(2,1)} %lin_h.1, bf16[8,8,128]{2,1,0:T(8,128)(2,1)} %stiff_h.1, f32[8,8,128]{2,1,0:T(8,128)} %anchor_h.1, s32[8,128]{1,0:T(8,128)} %bitcast.5, ...), custom_call_target="tpu_custom_call" | custom-call | tf_op jit(solution)/shard_map/pallas_call | solution.py:643
  33.1 0.7 %shard_map.96 = (f32[3,8,8,128]{3,2,1,0:T(8,128)}, f32[256,128]{1,0:T(8,128)}) custom-call(f32[3,3,8,8,128]{4,3,2,1,0:T(8,128)S(1)} %get-tuple-element.5.parts, f32[3,256,128]{2,1,0:T(8,128)S(1)} %get-tuple-element.6.tiles, f32[6,8,128]{2,1,0:T(8,128)S(1)} %get-tuple-element.7.factors), custom_call_target="tpu_custom_call" | custom-call | tf_op jit(solution)/shard_map/pallas_call | solution.py:673
